TPU v7x, 128 devices: a whole 4x4x4 slice. The times are simulated.
128 devices in a mesh: batch: 2 (over core), member: 16 (over y, x), tensor: 4 (over z).
Axes of the slice: x: 4, y: 4, z: 4, core: 2. Of those that a mesh axis runs over, the one named last changes fastest.
Arguments:
- rows_in: bfloat16 [2048, 1536], P(('batch', 'member', 'tensor')), may hold values from -6 to 6
- target: bfloat16 [2048, 1536], P(('batch', 'member'), 'tensor'), may hold values from -6 to 6
- w_in: bfloat16 [16, 1536, 4096], P('member', None, 'tensor'), may hold values from -0.15309311 to 0.15309311, as said below
- w_out: bfloat16 [16, 4096, 1536], P('member', 'tensor'), may hold values from -0.09375 to 0.09375, as said below
Outputs:
- reward: float32 [2048], P(('batch', 'member', 'tensor'))
- grad_in: float32 [16, 1536, 4096], P('member', 'batch', 'tensor')
- grad_out: float32 [16, 4096, 1536], P('member', 'tensor', 'batch')
Inputs may be any that keep to these rules, and one draw needn't show every extreme that they name: `w_in`: each entry lies within the stated bounds. `w_out`: each entry lies within the stated bounds.
All inputs are finite; a program needn't handle non-finite values.
Results may differ from a plain program's by a relative error of at most 0.0035.
The roundings to bfloat16 on the way count: a program that leaves them out, or rounds other values in their place, can miss the bound.
Values may be sent and summed in bfloat16 or wider, within the bound.
A program may use at most 128 MiB of HBM per device.

v0:
```python
import jax
import jax.numpy as jnp
from jax import lax
from jax.sharding import PartitionSpec as P


def silu_slope(pre_act):
    sigmoid = jax.nn.sigmoid(pre_act)
    return sigmoid * (1.0 + pre_act * (1.0 - sigmoid))


def per_device(rows_in, target, w_in, w_out):
    own_rows = rows_in.shape[0]
    gathered = lax.all_gather(rows_in, ("member", "tensor"), axis=0, tiled=True)
    targets_here = lax.all_gather(target, "member", axis=0, tiled=True)
    group_rows = gathered.shape[0]
    local_count = w_in.shape[0]
    members_all = local_count * lax.axis_size("member")
    width_all = w_out.shape[2]
    loss_scale = float(group_rows * lax.axis_size("batch")) ** (-0.5)
    pre_act = jnp.einsum("gf,mfh->mgh", gathered, w_in, preferred_element_type=jnp.float32)
    hidden = jax.nn.silu(pre_act).astype(jnp.bfloat16)
    partial_out = jnp.einsum("mgh,mhf->mgf", hidden, w_out, preferred_element_type=jnp.float32)
    predicted = lax.psum_scatter(partial_out, "tensor", scatter_dimension=2, tiled=True)
    errors = ((predicted - targets_here.astype(jnp.float32)[None]) * loss_scale).astype(
        jnp.bfloat16
    )
    errors_full = lax.all_gather(errors, "tensor", axis=2, tiled=True)
    own_block = lax.axis_index("member") * lax.axis_size("tensor") + lax.axis_index("tensor")
    summed = lax.psum(jnp.sum(predicted, 0).astype(jnp.bfloat16), "member").astype(jnp.float32)
    member_mean = summed / members_all
    spread = jnp.sum((predicted - member_mean[None]) ** 2, axis=(0, 2))
    spread = lax.psum(spread, ("member", "tensor"))
    reward_rows = spread / (members_all * width_all)
    reward = lax.dynamic_slice_in_dim(reward_rows, own_block * own_rows, own_rows, 0)
    grad_out_part = jnp.einsum(
        "mgh,mgf->mhf", hidden, errors_full, preferred_element_type=jnp.float32
    )
    back_grad = jnp.einsum("mgf,mhf->mgh", errors_full, w_out, preferred_element_type=jnp.float32)
    pre_grad = (back_grad * silu_slope(pre_act)).astype(jnp.bfloat16)
    grad_in_part = jnp.einsum("gf,mgh->mfh", gathered, pre_grad, preferred_element_type=jnp.float32)
    grad_in, grad_out = (
        lax.psum_scatter(grad_in_part, "batch", scatter_dimension=1, tiled=True),
        lax.psum_scatter(grad_out_part, "batch", scatter_dimension=2, tiled=True),
    )
    return (reward, grad_in, grad_out)


def solution(mesh):
    return jax.shard_map(
        per_device,
        mesh=mesh,
        in_specs=(
            P(("batch", "member", "tensor"), None),
            P(("batch", "member"), "tensor"),
            P("member", None, "tensor"),
            P("member", "tensor", None),
        ),
        out_specs=(
            P(("batch", "member", "tensor")),
            P("member", "batch", "tensor"),
            P("member", "tensor", "batch"),
        ),
        check_vma=False,
    )
```

profile of v0, /device:TPU:0, one launch (start us, length us, event | category | flops | bytes accessed | tf_op | source)
XLA Modules:
  0.0 499.6 jit_solution(12518371583038524889)
XLA Ops:
  7.2 0.0 copy-start
  7.2 0.0 all-gather.3.cloned.1.call-start
  7.2 0.7 all-gather.3.cloned.1.call-update
  7.9 0.0 reduce-scatter.4.cloned.1.call-start
  8.0 72.5 %all-gather.3.cloned.1.call-done = bf16[1024,1536]{1,0:T(8,128)(2,1)} async-done(((bf16[16,1536]{1,0:T(8,128)(2,1)}), bf16[1024,1536]{1,0:T(8,128)(2,1)}) %all-gather.3.cloned.1.call-update) | async-done | bytes 3145744 | tf_op jit(solution)/shard_map/all_gather | solution.py:14
  80.4 6.3 %fusion.12 = f32[1024,1024]{1,0:T(8,128)S(1)} fusion(bf16[1024,1536]{1,0:T(8,128)(2,1)} %all-gather.3.cloned.1.call-done, bf16[1,1536,1024]{2,1,0:T(8,128)(2,1)} %param.6), kind=kOutput, calls=%fused_computation.19 | convolution fusion | flops 3221225472 | bytes 10485760 | tf_op jit(solution)/shard_map/gf,mfh->mgh/dot_general | solution.py:21
  86.7 0.0 copy-start.2
  86.8 1.9 copy-done.2
  88.7 0.0 copy-done
  88.7 5.4 %convolution_bitcast_fusion.2 = f32[1,1024,1536]{2,1,0:T(8,128)} fusion(bf16[1,1024,1536]{2,1,0:T(8,128)(2,1)S(1)} %copy-done, f32[1024,1024]{1,0:T(8,128)S(1)} %fusion.12), kind=kOutput, calls=%fused_computation.2 | convolution fusion | flops 3226468352 | bytes 13631488 | tf_op jit(solution)/shard_map/mgh,mhf->mgf/dot_general | solution.py:23
  94.1 0.0 reduce-scatter.4.cloned.1.call-update
  94.1 0.0 copy-start.1
  94.1 0.0 all-reduce.2.cloned.1.call-start
  94.2 61.8 %reduce-scatter.4.cloned.1.call-done = f32[1,1024,384]{2,1,0:T(8,128)} async-done(((f32[1,1024,1536]{2,1,0:T(8,128)}), f32[1,1024,384]{2,1,0:T(8,128)}) %reduce-scatter.4.cloned.1.call-update) | async-done | bytes 1572880 | tf_op jit(solution)/shard_map/reduce_scatter | solution.py:24
  156.0 2.4 convert_bitcast_fusion
  158.4 0.0 all-reduce.2.cloned.1.call-update
  158.4 0.0 all-gather.5.cloned.1.call-start
  158.5 0.0 copy-done.1
  158.5 27.0 %all_gather.10 = bf16[1024,384]{1,0:T(8,128)(2,1)} all-gather(bf16[64,384]{1,0:T(8,128)(2,1)S(1)} %copy-done.1), channel_id=1, replica_groups=mesh['batch'=2,'member'=16,'tensor'=4] {'member'}, dimensions={0}, use_global_device_ids=true | all-gather | bytes 835584 | tf_op jit(solution)/shard_map/all_gather | solution.py:15
  185.4 60.7 %all-reduce.2.cloned.1.call-done = bf16[1024,384]{1,0:T(8,128)(2,1)} async-done(((bf16[1024,384]{1,0:T(8,128)(2,1)}), bf16[1024,384]{1,0:T(8,128)(2,1)}) %all-reduce.2.cloned.1.call-update) | async-done | bytes 786448 | tf_op jit(solution)/shard_map/psum | solution.py:30
  246.2 3.2 fusion.19
  249.3 0.0 all-gather.5.cloned.1.call-update
  249.4 0.0 reduce-scatter.6.cloned.1.call-start
  249.4 39.1 %all-gather.5.cloned.1.call-done = bf16[1,1024,1536]{2,1,0:T(8,128)(2,1)} async-done(((bf16[1,1024,384]{2,1,0:T(8,128)(2,1)}), bf16[1,1024,1536]{2,1,0:T(8,128)(2,1)}) %all-gather.5.cloned.1.call-update) | async-done | bytes 3145744 | tf_op jit(solution)/shard_map/all_gather | solution.py:28
  288.6 13.7 %convolution_bitcast_fusion.1 = f32[1,1536,1024]{1,2,0:T(8,128)} fusion(bf16[1024,1536]{1,0:T(8,128)(2,1)} %all-gather.3.cloned.1.call-done, f32[1024,1024]{1,0:T(8,128)} %copy-done.2, bf16[1,1024,1536]{2,1,0:T(8,128)(2,1)} %all-gather.5.cloned.1.call-done, bf16[1,1024,1536]{2,1,0:T(8,128)(2,1)S(1)} %copy-done), kind=kOutput, calls=%fused_computation.1 | convolution fusion | flops 6451888128 | bytes 19922944 | tf_op jit(solution)/shard_map/gf,mgh->mfh/dot_general | solution.py:41
  302.2 0.0 reduce-scatter.6.cloned.1.call-update
  302.3 0.2 reduce-scatter.8.cloned.1.call-start
  302.5 9.7 %convolution_bitcast_fusion = f32[1,1024,1536]{2,1,0:T(8,128)} fusion(bf16[1,1024,1536]{2,1,0:T(8,128)(2,1)} %all-gather.5.cloned.1.call-done, f32[1024,1024]{1,0:T(8,128)} %copy-done.2), kind=kOutput, calls=%fused_computation | convolution fusion | flops 3226468352 | bytes 13631488 | tf_op jit(solution)/shard_map/mgh,mgf->mhf/dot_general | solution.py:36
  312.2 0.0 reduce-scatter.8.cloned.1.call-update
  312.2 176.4 %psum.15 = f32[1024]{0:T(1024)S(1)} all-reduce(f32[1024]{0:T(1024)S(1)} %get-tuple-element.7), channel_id=1, replica_groups=mesh['batch'=2,'member'=16,'tensor'=4] {'member','tensor'}, use_global_device_ids=true, to_apply=%region_3.4 | all-reduce | flops 1024 | bytes 8192 | tf_op jit(solution)/shard_map/psum | solution.py:33
  488.6 0.6 dynamic_slice.3
  489.2 0.0 reduce-scatter.6.cloned.1.call-done
  489.2 3.5 copy.8
  492.7 0.0 reduce-scatter.8.cloned.1.call-done
  (1 shorter events, 0.0 us)
Async XLA Ops:
  7.2 81.5 %copy-start = (bf16[1,1024,1536]{2,1,0:T(8,128)(2,1)S(1)}, bf16[1,1024,1536]{2,1,0:T(8,128)(2,1)}, u32[]{:S(2)}) copy-start(bf16[1,1024,1536]{2,1,0:T(8,128)(2,1)} %param.7) | copy-start | bytes 9437188
  7.2 73.3 %all-gather.3.cloned.1.call-start = ((), (), s32[]{:S(2)}) async-start(), calls=%async_computation.3 | async-start | bytes 3194880 | tf_op jit(solution)/shard_map/all_gather | solution.py:14
  7.9 148.1 %reduce-scatter.4.cloned.1.call-start = ((), (), s32[]{:S(2)}) async-start(), calls=%async_computation.4 | async-start | bytes 7864320 | tf_op jit(solution)/shard_map/reduce_scatter | solution.py:24
  86.7 1.9 copy-start.2
  94.1 64.4 %copy-start.1 = (bf16[64,384]{1,0:T(8,128)(2,1)S(1)}, bf16[64,384]{1,0:T(8,128)(2,1)}, u32[]{:S(2)}) copy-start(bf16[64,384]{1,0:T(8,128)(2,1)} %param.5) | copy-start | bytes 147460
  94.1 152.0 %all-reduce.2.cloned.1.call-start = ((), (), s32[]{:S(2)}) async-start(), calls=%async_computation.5 | async-start | bytes 1572864 | tf_op jit(solution)/shard_map/psum | solution.py:30
  158.4 130.1 %all-gather.5.cloned.1.call-start = ((), (), s32[]{:S(2)}) async-start(), calls=%async_computation.6 | async-start | bytes 3932160 | tf_op jit(solution)/shard_map/all_gather | solution.py:28
  249.4 239.8 %reduce-scatter.6.cloned.1.call-start = ((), (), s32[]{:S(2)}) async-start(), calls=%async_computation.7 | async-start | bytes 9437184 | tf_op jit(solution)/shard_map/reduce_scatter | solution.py:43
  302.3 190.5 %reduce-scatter.8.cloned.1.call-start = ((), (), s32[]{:S(2)}) async-start(), calls=%async_computation.8 | async-start | bytes 9437184 | tf_op jit(solution)/shard_map/reduce_scatter | solution.py:44
Sparse Core Ops, SparseCore 0:
  10.9 69.5 all-gather.2
  94.3 61.7 reduce-scatter.3
  159.9 86.2 all-reduce.1
  249.5 39.0 all-gather.4
  302.4 17.1 reduce-scatter.5
  322.4 18.5 reduce-scatter.7
where the time goes:
time: 500 us
  waiting for transfers between devices  235 us (47%)
  blocking collectives  203 us (41%)
  matrix products  35.1 us (7%)
  between operations  14.2 us (3%)
  local copies, waits for them, and re-layouts  6.07 us (1%)
  other arithmetic  5.53 us (1%)
    psum x1, blocking collectives, per_device(): spread = lax.psum(spread, ('member', 'tensor'))  176 us
    all_gather x1, waiting for transfers between devices, per_device(): gathered = lax.all_gather(rows_in, ('member', 'tensor'), axis=0, tiled=True)  72.5 us
    reduce_scatter x1, waiting for transfers between devices, per_device(): lax.psum_scatter(partial_out, 'tensor', scatter_dimension=2, tiled=True)  61.8 us
    psum x1, waiting for transfers between devices, per_device(): lax.psum(jnp.sum(predicted, 0).astype(jnp.bfloat16), 'member')  60.7 us
    all_gather x1, waiting for transfers between devices, per_device(): errors_full = lax.all_gather(errors, 'tensor', axis=2, tiled=True)  39.1 us
    all_gather x1, blocking collectives, per_device(): targets_here = lax.all_gather(target, 'member', axis=0, tiled=True)  27 us
    dot_general x1, matrix products, per_device(): jnp.einsum('gf,mgh->mfh', gathered, pre_grad, preferred_element_type=jnp....  13.7 us
  transfers between devices with their start and end apart: 6, of which 4 were waited for; matrix products, arithmetic and copies ran while one was open for 3% of the time, Pallas kernels for 0%

commit v1 on v0

v1 whole, which is shorter than its diff:
```python
import jax
import jax.numpy as jnp
from jax import lax
from jax.experimental import pallas as pl
from jax.experimental.pallas import tpu as pltpu
from jax.sharding import PartitionSpec as P

MESH = pl.DeviceIdType.MESH
F32 = jnp.float32
BF16 = jnp.bfloat16

F = 1536
FH = F // 2
FQ = F // 4
HS = 1024
CH = 4
CR = 256
HALF = CR // 2
GR = CR // 4
W = F + FQ
MEMBERS = 16
SCALE = 2048.0**-0.5


def dot(a, b):
    return lax.dot_general(a, b, (((1,), (0,)), ((), ())), preferred_element_type=F32)


def dot_nt(a, b):
    return lax.dot_general(a, b, (((1,), (1,)), ((), ())), preferred_element_type=F32)


def dot_tn(a, b):
    return lax.dot_general(a, b, (((0,), (0,)), ((), ())), preferred_element_type=F32)


def kernel(
    rows_hbm, target_hbm, w_in_hbm, w_out_hbm,
    reward_ref, grad_in_hbm, grad_out_hbm,
    w_in, w_out, rows, rows_o, hid, slope, part, sbuf, rbuf, err, err_o, pre, acc_in, acc_out,
    pred_b, gathered, spread, spread_r,
    loc_sem, out_sem, zg_s, zg_r, p1_s, p1_r, p2_s, p2_r, rs_s, rs_r, ag_s, ag_r, core_s, core_r,
    rw_s, rw_r, rwl_sem, rz_s, rz_r,
):
    b = lax.axis_index("batch")
    m = lax.axis_index("member")
    t = lax.axis_index("tensor")
    y, x = m // 4, m % 4

    def z_dev(d):
        return (b, m, (t + d) % 4)

    def plane_dev(dy, dx):
        return (b, ((y + dy) % 4) * 4 + (x + dx) % 4, t)

    other = (1 - b, m, t)
    group_dev = [plane_dev(3, 0), plane_dev(1, 0), plane_dev(0, 3), plane_dev(0, 1)]

    def remote(src, dst, s, r, dev):
        return pltpu.make_async_remote_copy(
            src_ref=src, dst_ref=dst, send_sem=s, recv_sem=r, device_id=dev, device_id_type=MESH
        )

    def al(v, k):
        return pl.multiple_of(v, k)

    def quarter(q):
        return pl.ds(al((q % 4) * FQ, 128), FQ)

    mine_cols = pl.ds(al(b * FH, 128), FH)
    other_cols = pl.ds(al((1 - b) * FH, 128), FH)

    barrier = pltpu.get_barrier_semaphore()
    for d in range(1, 4):
        pl.semaphore_signal(barrier, inc=1, device_id=z_dev(d), device_id_type=MESH)
    pl.semaphore_signal(barrier, inc=1, device_id=other, device_id_type=MESH)

    @pl.loop(1, MEMBERS)
    def _(d):
        pl.semaphore_signal(
            barrier, inc=1, device_id=(b, (m + d) % MEMBERS, t), device_id_type=MESH
        )

    a_base = al(x * 32, 32)
    b_base = al(HALF + y * 32, 32)
    own_base = al(
        (1 - t // 2) * (x * 32 + t * 16) + (t // 2) * (HALF + y * 32 + (t - 2) * 16), 16
    )

    load_w_in = pltpu.make_async_copy(w_in_hbm.at[0], w_in, loc_sem.at[0])
    load_w_out = pltpu.make_async_copy(w_out_hbm.at[0], w_out, loc_sem.at[1])
    load_rows = pltpu.make_async_copy(
        rows_hbm, rows.at[0, pl.ds(own_base, 16), pl.ds(0, F)], loc_sem.at[2]
    )
    load_ta = pltpu.make_async_copy(
        target_hbm.at[pl.ds(0, 32)], rows.at[0, pl.ds(a_base, 32), pl.ds(F, FQ)], loc_sem.at[3]
    )
    load_tb = pltpu.make_async_copy(
        target_hbm.at[pl.ds(32, 32)], rows.at[0, pl.ds(b_base, 32), pl.ds(F, FQ)], loc_sem.at[4]
    )
    load_rows.start()
    load_ta.start()
    load_tb.start()

    pl.semaphore_wait(barrier, 3 + 1 + MEMBERS - 1)

    def z_gather(d):
        return remote(
            rows_hbm,
            rows.at[0, pl.ds(own_base, 16), pl.ds(0, F)],
            zg_s.at[d - 1],
            zg_r.at[d - 1],
            z_dev(d),
        )

    def z_gather_in(d):
        s = (t + 4 - d) % 4
        base = al((1 - s // 2) * (x * 32 + s * 16) + (s // 2) * (HALF + y * 32 + (s - 2) * 16), 16)
        return remote(
            rows_hbm,
            rows.at[0, pl.ds(base, 16), pl.ds(0, F)],
            zg_s.at[d - 1],
            zg_r.at[d - 1],
            z_dev(d),
        )

    for d in (2, 1, 3):
        z_gather(d).start()
    load_w_in.start()
    load_w_out.start()
    acc_in[...] = jnp.zeros_like(acc_in)
    acc_out[...] = jnp.zeros_like(acc_out)
    load_rows.wait()
    load_ta.wait()
    load_tb.wait()
    for d in (1, 3, 2):
        z_gather_in(d).wait_recv()

    def strip(axis, d):
        if axis == 0:
            return al(((x + d) % 4) * 32, 32)
        return al(HALF + ((y + d) % 4) * 32, 32)

    def axis_dev(axis, d):
        return plane_dev(0, d) if axis == 0 else plane_dev(d, 0)

    def phase1(axis, d):
        ref = rows.at[0, pl.ds(strip(axis, 0), 32)]
        k = axis * 4 + d // 2
        return remote(ref, ref, p1_s.at[k], p1_r.at[k], axis_dev(axis, d))

    def phase1_in(axis, d):
        ref = rows.at[0, pl.ds(strip(axis, 4 - d), 32)]
        k = axis * 4 + d // 2
        return remote(ref, ref, p1_s.at[k], p1_r.at[k], axis_dev(axis, d))

    def phase1_fwd(axis, d):
        ref = rows.at[0, pl.ds(al(strip(axis, 4 - d) + (d // 2) * 16, 16), 16)]
        k = axis * 4 + 2 + d // 2
        return remote(ref, ref, p1_s.at[k], p1_r.at[k], axis_dev(axis, d))

    def phase1_fwd_in(axis, d):
        ref = rows.at[0, pl.ds(al(strip(axis, 2) + (d // 2) * 16, 16), 16)]
        k = axis * 4 + 2 + d // 2
        return remote(ref, ref, p1_s.at[k], p1_r.at[k], axis_dev(axis, d))

    sides = [(0, 1), (0, 3), (1, 1), (1, 3)]
    for axis, d in sides:
        phase1(axis, d).start()
    for axis, d in sides:
        phase1_in(axis, d).wait_recv()
        phase1_fwd(axis, d).start()
    for axis, d in sides:
        phase1_fwd_in(axis, d).wait_recv()

    def phase2(c, g):
        src_chunk = 1 if c == 3 else 0
        src_group = g ^ 1 if c == 2 else g
        return remote(
            rows.at[src_chunk, pl.ds(src_group * GR, GR)],
            rows.at[c, pl.ds(g * GR, GR)],
            p2_s.at[c, g],
            p2_r.at[c, g],
            group_dev[g],
        )

    for c in (1, 2):
        for g in range(4):
            phase2(c, g).start()

    def core_copy(kind, c):
        src, dst = (
            (rows.at[c, :, other_cols], rows_o.at[c]),
            (hid.at[c, pl.ds(0, CR)], hid.at[c, pl.ds(CR, CR)]),
            (err.at[c, :, other_cols], err_o.at[c]),
            (pre.at[c, pl.ds(0, CR)], pre.at[c, pl.ds(CR, CR)]),
        )[kind]
        return remote(src, dst, core_s.at[kind, c], core_r.at[kind, c], other)

    def forward(c):
        core_copy(0, c).start()

        @pl.loop(0, HS // 256)
        def _(n):
            cols = pl.ds(al(n * 256, 256), 256)
            v = dot(rows[c, :, pl.ds(0, F)], w_in[:, cols])
            s = jax.nn.sigmoid(v)
            hid[c, pl.ds(0, CR), cols] = (v * s).astype(BF16)
            slope[c, :, cols] = s * (1.0 + v * (1.0 - s))

        core_copy(1, c).start()

        @pl.loop(0, 4)
        def _(k):
            rel = (3 + 2 * k - (k // 2)) % 4
            part[c, rel] = dot(hid[c, pl.ds(0, CR)], w_out[:, quarter(t + rel)])

            @pl.when(k == 0)
            def _():
                sbuf[c, 0, 0] = part[c, 3, pl.ds(0, HALF)].astype(BF16)
                rs(c, 0, 0).start()

            @pl.when(k == 1)
            def _():
                sbuf[c, 0, 1] = part[c, 1, pl.ds(HALF, HALF)].astype(BF16)
                rs(c, 0, 1).start()

    def rs(c, s, way):
        return remote(
            sbuf.at[c, s, way], rbuf.at[c, s, way], rs_s.at[c, s, way], rs_r.at[c, s, way],
            z_dev(1 if way == 0 else 3),
        )

    def rs_step(c, s):
        for way in range(2):
            rs(c, s - 1, way).wait_recv()
            rel = (3 - s) if way == 0 else (1 + s)
            own = part[c, rel, pl.ds(way * HALF, HALF)]
            sbuf[c, s, way] = (own + rbuf[c, s - 1, way].astype(F32)).astype(BF16)
            rs(c, s, way).start()

    def ag(c, way):
        ref = err.at[c, :, quarter(t)]
        return remote(ref, ref, ag_s.at[c, way], ag_r.at[c, way], z_dev(1 if way == 0 else 3))

    def ag_in(c, way):
        ref = err.at[c, :, quarter(t + (3 if way == 0 else 1))]
        return remote(ref, ref, ag_s.at[c, way], ag_r.at[c, way], z_dev(1 if way == 0 else 3))

    def ag_fwd(c, way):
        ref = err.at[c, pl.ds(way * HALF, HALF), quarter(t + (3 if way == 0 else 1))]
        k = 2 + way
        return remote(ref, ref, ag_s.at[c, k], ag_r.at[c, k], z_dev(1 if way == 0 else 3))

    def ag_fwd_in(c, way):
        ref = err.at[c, pl.ds(way * HALF, HALF), quarter(t + 2)]
        k = 2 + way
        return remote(ref, ref, ag_s.at[c, k], ag_r.at[c, k], z_dev(1 if way == 0 else 3))

    def reward_piece(c, p):
        first, second = (c + 1) // 2, (4 - (c + 1) // 2) % 4
        away = first if p % 4 < 2 else second
        idx = (p % 4 + 2 * ((c // 2) * (1 - c // 3))) % 4
        if p < 4:
            owner = ((y + away) % 4) * 4 + idx
        else:
            owner = idx * 4 + (x + away) % 4
        src = pred_b.at[c, pl.ds(32 * p, 32)]
        dst = gathered.at[m, pl.ds(32 * (p // 4), 32)]
        return owner, src, dst

    def reward_send(c):
        for p in range(8):
            owner, src, dst = reward_piece(c, p)

            @pl.when(owner != m)
            def _():
                remote(
                    src, dst, rw_s.at[c, p], rw_r.at[m, p // 4], (b, owner, t)
                ).start()

            @pl.when(owner == m)
            def _():
                pltpu.make_async_copy(src, dst, rwl_sem.at[p // 4]).start()

    def errors(c):
        for way in range(2):
            rs(c, 2, way).wait_recv()
            r = pl.ds(way * HALF, HALF)
            pred = part[c, 0, r] + rbuf[c, 2, way].astype(F32)
            goal = rows[c, r, pl.ds(F, FQ)].astype(F32)
            err[c, r, quarter(t)] = ((pred - goal) * SCALE).astype(BF16)
            pred_b[c, r] = pred.astype(BF16)
        ag(c, 0).start()
        ag(c, 1).start()
        reward_send(c)

    def ag_forward(c):
        for way in range(2):
            ag_in(c, way).wait_recv()
            ag_fwd(c, way).start()

    def back(c):
        for way in range(2):
            ag_fwd_in(c, way).wait_recv()
        core_copy(2, c).start()

        @pl.loop(0, HS // 256)
        def _(n):
            cols = pl.ds(al(n * 256, 256), 256)
            g = dot_nt(err[c], w_out[cols, :])
            pre[c, pl.ds(0, CR), cols] = (g * slope[c, :, cols]).astype(BF16)

        core_copy(3, c).start()

    def grads(c):
        core_copy(1, c).wait_recv()
        core_copy(2, c).wait_recv()

        @pl.loop(0, HS // 256)
        def _(n):
            cols = pl.ds(al(n * 256, 256), 256)
            acc_out[cols, :] += dot_tn(hid[c, pl.ds(0, CR), cols], err[c, :, mine_cols]) + dot_tn(
                hid[c, pl.ds(CR, CR), cols], err_o[c]
            )

        core_copy(0, c).wait_recv()
        core_copy(3, c).wait_recv()

        @pl.loop(0, FH // 256)
        def _(n):
            here = pl.ds(al(b * FH + n * 256, 128), 256)
            cols = pl.ds(al(n * 256, 256), 256)
            acc_in[cols, :] += dot_tn(rows[c, :, here], pre[c, pl.ds(0, CR)]) + dot_tn(
                rows_o[c, :, cols], pre[c, pl.ds(CR, CR)]
            )

    load_w_in.wait()
    load_w_out.wait()
    forward(0)

    def tick(i, carry):
        @pl.when(i >= 1)
        def _():
            errors(i - 1)

        @pl.when(i < CH)
        def _():
            rs_step(i, 1)

        @pl.when(i >= 2)
        def _():
            grads(i - 2)

        @pl.when(i >= 1)
        def _():
            ag_forward(i - 1)

        @pl.when(i < CH)
        def _():
            rs_step(i, 2)

        @pl.when(i < CH - 1)
        def _():
            for g in range(4):
                remote(
                    rows.at[0, pl.ds(0, GR)],
                    rows.at[i + 1, pl.ds(g * GR, GR)],
                    p2_s.at[i + 1, g],
                    p2_r.at[i + 1, g],
                    group_dev[g],
                ).wait_recv()

            @pl.when(i == 0)
            def _():
                for g in range(4):
                    phase2(3, g).start()

            forward(i + 1)

        @pl.when(i >= 1)
        def _():
            back(i - 1)

        return carry

    lax.fori_loop(0, CH + 1, tick, 0)

    def reward_in(s, half):
        return remote(
            pred_b.at[0, pl.ds(0, 32)],
            gathered.at[s, pl.ds(32 * half, 32)],
            rw_s.at[0, 0],
            rw_r.at[s, half],
            (b, s, t),
        )

    @pl.loop(0, MEMBERS)
    def _(s):
        @pl.when(s != m)
        def _():
            for half in range(2):
                reward_in(s, half).wait_recv()

        @pl.when(s == m)
        def _():
            for half in range(2):
                pltpu.make_async_copy(
                    pred_b.at[0, pl.ds(0, 32)],
                    gathered.at[s, pl.ds(32 * half, 32)],
                    rwl_sem.at[half],
                ).wait()

    total = jnp.zeros((64, 128), F32)
    for k in range(3):
        cols = pl.ds(128 * k, 128)
        mean = jnp.zeros((64, 128), F32)
        for s in range(MEMBERS):
            mean += gathered[s, :, cols].astype(F32)
        mean = mean * (1.0 / MEMBERS)
        for s in range(MEMBERS):
            dev = gathered[s, :, cols].astype(F32) - mean
            total += dev * dev
    spread[...] = total

    def spread_copy(d):
        return remote(
            spread.at[pl.ds(al(((t + d) % 4) * 16, 16), 16)],
            spread_r.at[d - 1],
            rz_s.at[d - 1],
            rz_r.at[d - 1],
            z_dev(d),
        )

    for d in range(1, 4):
        spread_copy(d).start()

    grads(CH - 1)
    out_in = pltpu.make_async_copy(acc_in, grad_in_hbm.at[0], out_sem.at[0])
    out_out = pltpu.make_async_copy(acc_out, grad_out_hbm.at[0], out_sem.at[1])
    out_in.start()
    out_out.start()

    for d in range(1, 4):
        spread_copy(d).wait_recv()
    own = spread[pl.ds(al(t * 16, 16), 16)]
    for d in range(3):
        own += spread_r[d]
    reward_ref[...] = jnp.sum(own, axis=1, keepdims=True) * (1.0 / (MEMBERS * F))

    for d in range(1, 4):
        z_gather(d).wait_send()
        spread_copy(d).wait_send()
    for axis, d in sides:
        phase1(axis, d).wait_send()
        phase1_fwd(axis, d).wait_send()
    for c in (1, 2, 3):
        for g in range(4):
            phase2(c, g).wait_send()

    @pl.loop(0, CH)
    def _(c):
        for way in range(2):
            for s in range(3):
                rs(c, s, way).wait_send()
            ag(c, way).wait_send()
            ag_fwd(c, way).wait_send()
        for kind in range(4):
            core_copy(kind, c).wait_send()
        for p in range(8):
            owner, src, dst = reward_piece(c, p)

            @pl.when(owner != m)
            def _():
                remote(src, dst, rw_s.at[c, p], rw_r.at[m, p // 4], (b, owner, t)).wait_send()

    out_in.wait()
    out_out.wait()


def per_device(rows_in, target, w_in, w_out):
    any_spec = pl.BlockSpec(memory_space=pl.ANY)
    vmem = pltpu.VMEM
    dma = pltpu.SemaphoreType.DMA
    reward, grad_in, grad_out = pl.pallas_call(
        kernel,
        out_shape=(
            jax.ShapeDtypeStruct((16, 1), F32),
            jax.ShapeDtypeStruct((1, FH, HS), F32),
            jax.ShapeDtypeStruct((1, HS, FH), F32),
        ),
        in_specs=[any_spec] * 4,
        out_specs=(pl.BlockSpec(memory_space=pltpu.VMEM), any_spec, any_spec),
        scratch_shapes=[
            vmem((F, HS), BF16),
            vmem((HS, F), BF16),
            vmem((CH, CR, W), BF16),
            vmem((CH, CR, FH), BF16),
            vmem((CH, 2 * CR, HS), BF16),
            vmem((CH, CR, HS), F32),
            vmem((CH, 4, CR, FQ), F32),
            vmem((CH, 3, 2, HALF, FQ), BF16),
            vmem((CH, 3, 2, HALF, FQ), BF16),
            vmem((CH, CR, F), BF16),
            vmem((CH, CR, FH), BF16),
            vmem((CH, 2 * CR, HS), BF16),
            vmem((FH, HS), F32),
            vmem((HS, FH), F32),
            vmem((CH, CR, FQ), BF16),
            vmem((MEMBERS, 64, FQ), BF16),
            vmem((64, 128), F32),
            vmem((3, 16, 128), F32),
            dma((5,)),
            dma((2,)),
            dma((3,)),
            dma((3,)),
            dma((8,)),
            dma((8,)),
            dma((4, 4)),
            dma((4, 4)),
            dma((CH, 3, 2)),
            dma((CH, 3, 2)),
            dma((CH, 4)),
            dma((CH, 4)),
            dma((4, CH)),
            dma((4, CH)),
            dma((CH, 8)),
            dma((MEMBERS, 2)),
            dma((2,)),
            dma((3,)),
            dma((3,)),
        ],
        compiler_params=pltpu.CompilerParams(
            collective_id=0, has_side_effects=True, vmem_limit_bytes=60 * 1024 * 1024
        ),
        name="ensemble",
    )(rows_in, target, w_in, w_out)
    return reward.reshape(16), grad_in, grad_out


def solution(mesh):
    return jax.shard_map(
        per_device,
        mesh=mesh,
        in_specs=(
            P(("batch", "member", "tensor"), None),
            P(("batch", "member"), "tensor"),
            P("member", None, "tensor"),
            P("member", "tensor", None),
        ),
        out_specs=(
            P(("batch", "member", "tensor")),
            P("member", "batch", "tensor"),
            P("member", "tensor", "batch"),
        ),
        check_vma=False,
    )
```

time: 500 us -> 105 us (0.21)
  waiting for transfers between devices: 235 us -> 0 us
  blocking collectives: 203 us -> 0 us
  Pallas kernels: 0 us -> 96.3 us
  matrix products: 35.1 us -> 0 us
  between operations: 14.2 us -> 0.64 us
    psum x1 -> x0, blocking collectives: 176 us -> none  [per_device(): spread = lax.psum(spread, ('member', 'tensor'))]
    all_gather x2 -> x0, waiting for transfers between devices: 112 us -> none  [the longest x1 72.5 us: per_device(): gathered = lax.all_gather(rows_in, ('member', 'tensor'), axis=0, tiled=True)]
    pallas_call x0 -> x1, Pallas kernels: none -> 96.3 us  [per_device(): pl.pallas_call(kernel, out_shape=(jax.ShapeDtypeStruct((16, 1), F32), jax...]
    reduce_scatter x3 -> x0, waiting for transfers between devices: 61.8 us -> none  [the longest x1 61.8 us: per_device(): lax.psum_scatter(partial_out, 'tensor', scatter_dimension=2, tiled=True)]
    psum x1 -> x0, waiting for transfers between devices: 60.7 us -> none  [per_device(): lax.psum(jnp.sum(predicted, 0).astype(jnp.bfloat16), 'member')]
    dot_general x4 -> x0, matrix products: 35.1 us -> none  [the longest x1 13.7 us: per_device(): jnp.einsum('gf,mgh->mfh', gathered, pre_grad, preferred_element_type=jnp....]
    all_gather x1 -> x0, blocking collectives: 27 us -> none  [per_device(): targets_here = lax.all_gather(target, 'member', axis=0, tiled=True)]
    convert_element_type x2 -> x0, other arithmetic: 5.53 us -> none  [the longest x1 3.16 us: per_device(): ((predicted - targets_here.astype(jnp.float32)[None]) * loss_scale).astyp...]
  transfers between devices with their start and end apart: 6 -> 0, of which waited for: 4 -> 0; matrix products, arithmetic and copies ran while one was open for 3% -> 0% of each run, Pallas kernels for 0% -> 0%
where the time goes in v1:
time: 105 us; the launch traced here: 104 us
  Pallas kernels  96.3 us (92%)
  local copies, waits for them, and re-layouts  5.79 us (6%)
  other arithmetic  1.32 us (1%)
    pallas_call x1, Pallas kernels, per_device(): pl.pallas_call(kernel, out_shape=(jax.ShapeDtypeStruct((16, 1), F32), jax...  96.3 us
    unnamed x4, local copies, waits for them, and re-layouts  5.79 us

profile of v1, /device:TPU:0, one launch (start us, length us, event | category | flops | bytes accessed | tf_op | source)
XLA Modules:
  0.0 104.1 jit_solution(16480869842948989243)
XLA Ops:
  0.6 96.3 %ensemble.1 = (f32[16,1]{1,0:T(8,128)}, f32[1,768,1024]{2,1,0:T(8,128)}, f32[1,1024,768]{2,1,0:T(8,128)}) custom-call(bf16[16,1536]{1,0:T(8,128)(2,1)} %rows_hbm.1, bf16[64,384]{1,0:T(8,128)(2,1)} %target_hbm.1, bf16[1,1536,1024]{2,1,0:T(8,128)(2,1)} %w_in_hbm.1, bf16[1,1024,1536]{2,1,0:T(8,128)(2,1)} %w_out_hbm.1), custom_call_target="tpu_custom_call" | custom-call | tf_op jit(solution)/shard_map/ensemble/pallas_call | solution.py:485
  97.0 1.3 %reduce = f32[16]{0:T(128)} reduce(f32[16,1]{1,0:T(8,128)} %get-tuple-element.6, f32[]{:T(128)} %constant.3), dimensions={1}, to_apply=%get-tuple-element.6.reduce_sub_computation | reduce | bytes 132 | tf_op jit(solution)/shard_map/ensemble/pallas_call | solution.py:485
  98.3 0.0 copy-start
  98.3 4.1 %copy.9 = f32[1,768,1024]{2,1,0:T(8,128)} copy(f32[1,768,1024]{2,1,0:T(8,128)} %get-tuple-element.13) | data formatting | bytes 6291456
  102.4 0.0 copy-done
  102.4 1.7 %copy.10 = f32[1,1024,768]{2,1,0:T(8,128)} copy(f32[1,1024,768]{2,1,0:T(8,128)S(1)} %copy-done) | data formatting | bytes 6291456
Async XLA Ops:
  98.3 4.1 %copy-start = (f32[1,1024,768]{2,1,0:T(8,128)S(1)}, f32[1,1024,768]{2,1,0:T(8,128)}, u32[]{:S(2)}) copy-start(f32[1,1024,768]{2,1,0:T(8,128)} %get-tuple-element.14) | copy-start | bytes 9437188

commit v2 on v1

--- a/solution.py
+++ b/solution.py
@@ -36,10 +36,10 @@
 
 def kernel(
     rows_hbm, target_hbm, w_in_hbm, w_out_hbm,
-    reward_ref, grad_in_hbm, grad_out_hbm,
-    w_in, w_out, rows, rows_o, hid, slope, part, sbuf, rbuf, err, err_o, pre, acc_in, acc_out,
+    reward_ref, acc_in, acc_out,
+    w_in, w_out, rows, rows_o, hid, slope, part, sbuf, rbuf, err, err_o, pre,
     pred_b, gathered, spread, spread_r,
-    loc_sem, out_sem, zg_s, zg_r, p1_s, p1_r, p2_s, p2_r, rs_s, rs_r, ag_s, ag_r, core_s, core_r,
+    loc_sem, zg_s, zg_r, p1_s, p1_r, p2_s, p2_r, rs_s, rs_r, ag_s, ag_r, core_s, core_r,
     rw_s, rw_r, rwl_sem, rz_s, rz_r,
 ):
     b = lax.axis_index("batch")
@@ -101,6 +101,8 @@
     load_rows.start()
     load_ta.start()
     load_tb.start()
+    load_w_in.start()
+    load_w_out.start()
 
     pl.semaphore_wait(barrier, 3 + 1 + MEMBERS - 1)
 
@@ -126,8 +128,6 @@
 
     for d in (2, 1, 3):
         z_gather(d).start()
-    load_w_in.start()
-    load_w_out.start()
     acc_in[...] = jnp.zeros_like(acc_in)
     acc_out[...] = jnp.zeros_like(acc_out)
     load_rows.wait()
@@ -200,7 +200,7 @@
     def forward(c):
         core_copy(0, c).start()
 
-        @pl.loop(0, HS // 256)
+        @pl.loop(0, HS // 256, unroll=True)
         def _(n):
             cols = pl.ds(al(n * 256, 256), 256)
             v = dot(rows[c, :, pl.ds(0, F)], w_in[:, cols])
@@ -209,21 +209,16 @@
             slope[c, :, cols] = s * (1.0 + v * (1.0 - s))
 
         core_copy(1, c).start()
-
-        @pl.loop(0, 4)
-        def _(k):
-            rel = (3 + 2 * k - (k // 2)) % 4
+        for rel in (3, 1, 2, 0):
             part[c, rel] = dot(hid[c, pl.ds(0, CR)], w_out[:, quarter(t + rel)])
-
-            @pl.when(k == 0)
-            def _():
+            if rel == 3:
                 sbuf[c, 0, 0] = part[c, 3, pl.ds(0, HALF)].astype(BF16)
-                rs(c, 0, 0).start()
-
-            @pl.when(k == 1)
-            def _():
+            elif rel == 1:
                 sbuf[c, 0, 1] = part[c, 1, pl.ds(HALF, HALF)].astype(BF16)
-                rs(c, 0, 1).start()
+
+    def rs_start(c):
+        rs(c, 0, 0).start()
+        rs(c, 0, 1).start()
 
     def rs(c, s, way):
         return remote(
@@ -293,7 +288,6 @@
             pred_b[c, r] = pred.astype(BF16)
         ag(c, 0).start()
         ag(c, 1).start()
-        reward_send(c)
 
     def ag_forward(c):
         for way in range(2):
@@ -305,7 +299,7 @@
             ag_fwd_in(c, way).wait_recv()
         core_copy(2, c).start()
 
-        @pl.loop(0, HS // 256)
+        @pl.loop(0, HS // 256, unroll=True)
         def _(n):
             cols = pl.ds(al(n * 256, 256), 256)
             g = dot_nt(err[c], w_out[cols, :])
@@ -317,48 +311,39 @@
         core_copy(1, c).wait_recv()
         core_copy(2, c).wait_recv()
 
-        @pl.loop(0, HS // 256)
+        @pl.loop(0, HS // 256, unroll=True)
         def _(n):
             cols = pl.ds(al(n * 256, 256), 256)
-            acc_out[cols, :] += dot_tn(hid[c, pl.ds(0, CR), cols], err[c, :, mine_cols]) + dot_tn(
+            acc_out[0, cols, :] += dot_tn(hid[c, pl.ds(0, CR), cols], err[c, :, mine_cols]) + dot_tn(
                 hid[c, pl.ds(CR, CR), cols], err_o[c]
             )
 
         core_copy(0, c).wait_recv()
         core_copy(3, c).wait_recv()
 
-        @pl.loop(0, FH // 256)
+        @pl.loop(0, FH // 256, unroll=True)
         def _(n):
             here = pl.ds(al(b * FH + n * 256, 128), 256)
             cols = pl.ds(al(n * 256, 256), 256)
-            acc_in[cols, :] += dot_tn(rows[c, :, here], pre[c, pl.ds(0, CR)]) + dot_tn(
+            acc_in[0, cols, :] += dot_tn(rows[c, :, here], pre[c, pl.ds(0, CR)]) + dot_tn(
                 rows_o[c, :, cols], pre[c, pl.ds(CR, CR)]
             )
 
     load_w_in.wait()
     load_w_out.wait()
     forward(0)
+    rs_start(0)
 
     def tick(i, carry):
         @pl.when(i >= 1)
         def _():
             errors(i - 1)
 
-        @pl.when(i < CH)
-        def _():
-            rs_step(i, 1)
-
         @pl.when(i >= 2)
         def _():
-            grads(i - 2)
-
-        @pl.when(i >= 1)
-        def _():
-            ag_forward(i - 1)
-
-        @pl.when(i < CH)
-        def _():
-            rs_step(i, 2)
+            back(i - 2)
+
+        rs_step(i, 1)
 
         @pl.when(i < CH - 1)
         def _():
@@ -378,13 +363,68 @@
 
             forward(i + 1)
 
+            @pl.when(i == 0)
+            def _():
+                rs_start(1)
+
         @pl.when(i >= 1)
         def _():
-            back(i - 1)
+            ag_forward(i - 1)
+
+        rs_step(i, 2)
+
+        @pl.when((i >= 1) & (i < CH - 1))
+        def _():
+            rs_start(i + 1)
+
+        @pl.when(i >= 1)
+        def _():
+            reward_send(i - 1)
+
+        @pl.when(i >= 2)
+        def _():
+            grads(i - 2)
 
         return carry
 
-    lax.fori_loop(0, CH + 1, tick, 0)
+    lax.fori_loop(0, CH, tick, 0)
+    errors(CH - 1)
+    back(CH - 2)
+    reward_send(CH - 1)
+    grads(CH - 2)
+    ag_forward(CH - 1)
+
+    for d in range(1, 4):
+        z_gather(d).wait_send()
+    for axis, d in sides:
+        phase1(axis, d).wait_send()
+        phase1_fwd(axis, d).wait_send()
+    for c in (1, 2, 3):
+        for g in range(4):
+            phase2(c, g).wait_send()
+
+    def sent(c, last):
+        for way in range(2):
+            for s in range(3):
+                rs(c, s, way).wait_send()
+            ag(c, way).wait_send()
+            if not last:
+                ag_fwd(c, way).wait_send()
+        for kind in range(4):
+            if not (last and kind >= 2):
+                core_copy(kind, c).wait_send()
+        for p in range(8):
+            owner, src, dst = reward_piece(c, p)
+
+            @pl.when(owner != m)
+            def _():
+                remote(src, dst, rw_s.at[c, p], rw_r.at[m, p // 4], (b, owner, t)).wait_send()
+
+    @pl.loop(0, CH - 1)
+    def _(c):
+        sent(c, False)
+
+    sent(CH - 1, True)
 
     def reward_in(s, half):
         return remote(
@@ -435,47 +475,22 @@
     for d in range(1, 4):
         spread_copy(d).start()
 
+    back(CH - 1)
     grads(CH - 1)
-    out_in = pltpu.make_async_copy(acc_in, grad_in_hbm.at[0], out_sem.at[0])
-    out_out = pltpu.make_async_copy(acc_out, grad_out_hbm.at[0], out_sem.at[1])
-    out_in.start()
-    out_out.start()
 
     for d in range(1, 4):
         spread_copy(d).wait_recv()
     own = spread[pl.ds(al(t * 16, 16), 16)]
     for d in range(3):
         own += spread_r[d]
-    reward_ref[...] = jnp.sum(own, axis=1, keepdims=True) * (1.0 / (MEMBERS * F))
+    reward_ref[...] = jnp.sum(own.T, axis=0, keepdims=True) * (1.0 / (MEMBERS * F))
 
     for d in range(1, 4):
-        z_gather(d).wait_send()
         spread_copy(d).wait_send()
-    for axis, d in sides:
-        phase1(axis, d).wait_send()
-        phase1_fwd(axis, d).wait_send()
-    for c in (1, 2, 3):
-        for g in range(4):
-            phase2(c, g).wait_send()
-
-    @pl.loop(0, CH)
-    def _(c):
-        for way in range(2):
-            for s in range(3):
-                rs(c, s, way).wait_send()
-            ag(c, way).wait_send()
-            ag_fwd(c, way).wait_send()
-        for kind in range(4):
-            core_copy(kind, c).wait_send()
-        for p in range(8):
-            owner, src, dst = reward_piece(c, p)
-
-            @pl.when(owner != m)
-            def _():
-                remote(src, dst, rw_s.at[c, p], rw_r.at[m, p // 4], (b, owner, t)).wait_send()
-
-    out_in.wait()
-    out_out.wait()
+    for way in range(2):
+        ag_fwd(CH - 1, way).wait_send()
+    for kind in (2, 3):
+        core_copy(kind, CH - 1).wait_send()
 
 
 def per_device(rows_in, target, w_in, w_out):
@@ -485,12 +500,12 @@
     reward, grad_in, grad_out = pl.pallas_call(
         kernel,
         out_shape=(
-            jax.ShapeDtypeStruct((16, 1), F32),
-            jax.ShapeDtypeStruct((1, FH, HS), F32),
-            jax.ShapeDtypeStruct((1, HS, FH), F32),
+            vmem((1, 16), F32),
+            vmem((1, FH, HS), F32),
+            vmem((1, HS, FH), F32),
         ),
         in_specs=[any_spec] * 4,
-        out_specs=(pl.BlockSpec(memory_space=pltpu.VMEM), any_spec, any_spec),
+        out_specs=(pl.BlockSpec(memory_space=pltpu.VMEM),) * 3,
         scratch_shapes=[
             vmem((F, HS), BF16),
             vmem((HS, F), BF16),
@@ -504,14 +519,11 @@
             vmem((CH, CR, F), BF16),
             vmem((CH, CR, FH), BF16),
             vmem((CH, 2 * CR, HS), BF16),
-            vmem((FH, HS), F32),
-            vmem((HS, FH), F32),
             vmem((CH, CR, FQ), BF16),
             vmem((MEMBERS, 64, FQ), BF16),
             vmem((64, 128), F32),
             vmem((3, 16, 128), F32),
             dma((5,)),
-            dma((2,)),
             dma((3,)),
             dma((3,)),
             dma((8,)),
@@ -531,7 +543,7 @@
             dma((3,)),
         ],
         compiler_params=pltpu.CompilerParams(
-            collective_id=0, has_side_effects=True, vmem_limit_bytes=60 * 1024 * 1024
+            collective_id=0, has_side_effects=True, vmem_limit_bytes=54 * 1024 * 1024
         ),
         name="ensemble",
     )(rows_in, target, w_in, w_out)

time: 105 us -> 96.7 us (0.921)
  Pallas kernels: 96.3 us -> 90.3 us
  local copies, waits for them, and re-layouts: 5.79 us -> 3.84 us
  other arithmetic: 1.32 us -> 0 us
    pallas_call x1, Pallas kernels: 96.3 us -> 90.3 us  [per_device(): pl.pallas_call(kernel, out_shape=(vmem((1, 16), F32), vmem((1, FH, HS), F...]
    unnamed x4 -> x3, local copies, waits for them, and re-layouts: 5.79 us -> 3.84 us
    pallas_call x1 -> x0, other arithmetic: 1.32 us -> none  [per_device(): pl.pallas_call(kernel, out_shape=(jax.ShapeDtypeStruct((16, 1), F32), jax...]
where the time goes in v2:
time: 96.7 us; the launch traced here: 94.8 us
  Pallas kernels  90.3 us (93%)
  local copies, waits for them, and re-layouts  3.84 us (4%)
    pallas_call x1, Pallas kernels, per_device(): pl.pallas_call(kernel, out_shape=(vmem((1, 16), F32), vmem((1, FH, HS), F...  90.3 us
    unnamed x3, local copies, waits for them, and re-layouts  3.84 us

profile of v2, /device:TPU:0, one launch (start us, length us, event | category | flops | bytes accessed | tf_op | source)
XLA Modules:
  0.0 94.8 jit_solution(13220457797969829214)
XLA Ops:
  0.6 90.3 %ensemble.1 = (f32[1,16]{1,0:T(1,128)S(1)}, f32[1,768,1024]{2,1,0:T(8,128)S(1)}, f32[1,1024,768]{2,1,0:T(8,128)S(1)}) custom-call(bf16[16,1536]{1,0:T(8,128)(2,1)} %rows_hbm.1, bf16[64,384]{1,0:T(8,128)(2,1)} %target_hbm.1, bf16[1,1536,1024]{2,1,0:T(8,128)(2,1)} %w_in_hbm.1, bf16[1,1024,1536]{2,1,0:T(8,128)(2,1)} %w_out_hbm.1), custom_call_target="tpu_custom_call" | custom-call | tf_op jit(solution)/shard_map/ensemble/pallas_call | solution.py:500
  90.9 0.5 copy.10
  91.4 1.7 %copy.11 = f32[1,768,1024]{2,1,0:T(8,128)} copy(f32[1,768,1024]{2,1,0:T(8,128)S(1)} %get-tuple-element.10) | data formatting | bytes 6291456
  93.1 1.7 %copy.12 = f32[1,1024,768]{2,1,0:T(8,128)} copy(f32[1,1024,768]{2,1,0:T(8,128)S(1)} %get-tuple-element.11) | data formatting | bytes 6291456

commit v3 on v0

v3 whole, which is shorter than its diff:
```python
import jax
import jax.numpy as jnp
from jax import lax
from jax.experimental import pallas as pl
from jax.experimental.pallas import tpu as pltpu
from jax.sharding import PartitionSpec as P

MESH = pl.DeviceIdType.MESH
F32 = jnp.float32
BF16 = jnp.bfloat16

F = 1536
FH = F // 2
FQ = F // 4
HS = 1024
R = 1024
W = F + FQ
ST = 32
MEMBERS = 16
SCALE = 2048.0**-0.5

CHUNKS = (
    ("A00", "B00"),
    ("A01", "A03", "B10", "B30"),
    ("A10", "A30", "B01", "B03"),
    ("A11", "A13", "A31", "A33", "B11", "B31", "B13", "B33"),
    ("A02", "A12", "A32", "B20", "B21", "B23"),
    ("A20", "A23", "B02", "B32"),
    ("A21", "A22", "B12", "B22"),
)
STRIPS = tuple(s for chunk in CHUNKS for s in chunk)
POS = {s: ST * k for k, s in enumerate(STRIPS)}
SIZE = tuple(ST * len(chunk) for chunk in CHUNKS)
OFF = tuple(sum(SIZE[:c]) for c in range(len(CHUNKS)))
NC = len(CHUNKS)
GROUPS = ((0, 1, 2), (3,), (4,), (5, 6))
NG = len(GROUPS)

HOPS = (
    ("p1", "A00", 0, 32, "A03", (0, 1)),
    ("p1", "A00", 0, 32, "A01", (0, 3)),
    ("p1", "B00", 0, 32, "B30", (1, 0)),
    ("p1", "B00", 0, 32, "B10", (3, 0)),
    ("p2", "A00", 0, 32, "A30", (1, 0)),
    ("p2", "A00", 0, 32, "A10", (3, 0)),
    ("p2", "B00", 0, 32, "B03", (0, 1)),
    ("p2", "B00", 0, 32, "B01", (0, 3)),
    ("d", "A03", 0, 16, "A02", (0, 1)),
    ("d", "A01", 16, 16, "A02", (0, 3)),
    ("d", "B30", 0, 16, "B20", (1, 0)),
    ("d", "B10", 16, 16, "B20", (3, 0)),
    ("q3", "A01", 0, 64, "A31", (1, 0)),
    ("q3", "A01", 0, 64, "A11", (3, 0)),
    ("q3", "B10", 0, 64, "B13", (0, 1)),
    ("q3", "B10", 0, 64, "B11", (0, 3)),
    ("q4", "A02", 0, 32, "A32", (1, 0)),
    ("q4", "A02", 0, 32, "A12", (3, 0)),
    ("q4", "B20", 0, 32, "B23", (0, 1)),
    ("q4", "B20", 0, 32, "B21", (0, 3)),
    ("q5", "A33", 0, 32, "A23", (1, 0)),
    ("q5", "A10", 0, 32, "A20", (3, 0)),
    ("q5", "B33", 0, 32, "B32", (0, 1)),
    ("q5", "B01", 0, 32, "B02", (0, 3)),
    ("q6", "A32", 0, 32, "A22", (1, 0)),
    ("q6", "A11", 0, 32, "A21", (3, 0)),
    ("q6", "B23", 0, 32, "B22", (0, 1)),
    ("q6", "B11", 0, 32, "B12", (0, 3)),
)
NEEDS = ((), ("p1",), ("p2",), ("q3",), ("d", "q4"), ("q5",), ("q6",))
RELAY = {
    "X1": (("p1",), ("d", "q3")),
    "X2": (("d",), ("q4",)),
    "X3": (("p2", "q3"), ("q5",)),
    "X4": (("q3", "q4"), ("q6",)),
}
ORDER = (
    "P1", "F0", "G0", "H0", "R0", "X1", "F1", "G1", "S0", "F2", "G2", "H2", "H1", "R1", "X2",
    "E0", "R2", "S1", "A0", "F3", "S2", "X3", "G3", "E1", "F4", "E2", "G4", "H3", "F5", "X4",
    "H5", "H4", "G5", "W1", "R3", "A2", "R4", "F6", "A1", "H6", "S3", "G6", "W2", "S4", "R5",
    "B0", "E3", "W0", "R6", "A3", "S5", "I0", "S6", "E4", "O0", "E5", "W5", "E6", "B1", "A4",
    "W4", "W3", "A5", "O1", "A6", "W6", "I1", "B2", "T1", "B3", "Y1", "O2", "I2", "I3", "O3",
    "Y2",
)


def dot(a, b):
    return lax.dot_general(a, b, (((1,), (0,)), ((), ())), preferred_element_type=F32)


def dot_nt(a, b):
    return lax.dot_general(a, b, (((1,), (1,)), ((), ())), preferred_element_type=F32)


def dot_tn(a, b):
    return lax.dot_general(a, b, (((0,), (0,)), ((), ())), preferred_element_type=F32)


def kernel(
    rows_hbm, target_hbm, w_in_hbm, w_out_hbm,
    reward_ref, acc_in, acc_out,
    w_in, w_out, rows, rows_o, hid, slope, part, sbuf, rbuf, err, err_o, pre,
    pred_b, gathered, spread, spread_r,
    loc_sem, zg_s, zg_r, xy_s, xy_r, rs_s, rs_r, ag_s, ag_r, core_s, core_r, grp_s, grp_r,
    rw_s, rw_r, rwl_sem, rz_s, rz_r,
):
    b = lax.axis_index("batch")
    m = lax.axis_index("member")
    t = lax.axis_index("tensor")
    y, x = m // 4, m % 4

    def z_dev(d):
        return (b, m, (t + d) % 4)

    def plane_dev(dy, dx):
        return (b, ((y + dy) % 4) * 4 + (x + dx) % 4, t)

    other = (1 - b, m, t)

    def remote(src, dst, s, r, dev):
        return pltpu.make_async_remote_copy(
            src_ref=src, dst_ref=dst, send_sem=s, recv_sem=r, device_id=dev, device_id_type=MESH
        )

    started = []

    def go(copy):
        copy.start()
        started.append(copy)

    def al(v, k):
        return pl.multiple_of(v, k)

    def quarter(q):
        return pl.ds(al((q % 4) * FQ, 128), FQ)

    mine_cols = pl.ds(al(b * FH, 128), FH)
    other_cols = pl.ds(al((1 - b) * FH, 128), FH)

    barrier = pltpu.get_barrier_semaphore()
    for d in range(1, 4):
        pl.semaphore_signal(barrier, inc=1, device_id=z_dev(d), device_id_type=MESH)
    pl.semaphore_signal(barrier, inc=1, device_id=other, device_id_type=MESH)

    @pl.loop(1, MEMBERS)
    def _(d):
        pl.semaphore_signal(
            barrier, inc=1, device_id=(b, (m + d) % MEMBERS, t), device_id_type=MESH
        )

    own_rows = rows.at[pl.ds(al(t * 16, 16), 16), pl.ds(0, F)]
    load_rows = pltpu.make_async_copy(rows_hbm, own_rows, loc_sem.at[0])
    load_target = pltpu.make_async_copy(
        target_hbm, rows.at[pl.ds(0, 64), pl.ds(F, FQ)], loc_sem.at[1]
    )
    load_w_in = pltpu.make_async_copy(w_in_hbm.at[0], w_in, loc_sem.at[2])
    load_w_out = pltpu.make_async_copy(w_out_hbm.at[0], w_out, loc_sem.at[3])
    load_rows.start()
    load_target.start()
    load_w_in.start()
    load_w_out.start()
    pl.semaphore_wait(barrier, 3 + 1 + MEMBERS - 1)

    for d in (2, 1, 3):
        go(remote(rows_hbm, own_rows, zg_s.at[d - 1], zg_r.at[d - 1], z_dev(d)))
    load_rows.wait()
    load_target.wait()
    for d in (1, 3, 2):
        theirs = rows.at[pl.ds(al(((t + 4 - d) % 4) * 16, 16), 16), pl.ds(0, F)]
        remote(rows_hbm, theirs, zg_s.at[d - 1], zg_r.at[d - 1], z_dev(d)).wait_recv()

    def hop(k):
        _, first, skip, n, land, (dy, dx) = HOPS[k]
        return remote(
            rows.at[pl.ds(POS[first] + skip, n)],
            rows.at[pl.ds(POS[land] + skip, n)],
            xy_s.at[k],
            xy_r.at[k],
            plane_dev(dy, dx),
        )

    here = set()

    def arrived(names):
        for name in names:
            if name not in here:
                here.add(name)
                for k in range(len(HOPS)):
                    if HOPS[k][0] == name:
                        hop(k).wait_recv()

    def send_hops(names):
        for name in names:
            for k in range(len(HOPS)):
                if HOPS[k][0] == name:
                    go(hop(k))

    def core_copy(kind, c):
        r = pl.ds(OFF[c], SIZE[c])
        if kind == 0:
            src, dst = rows.at[r, other_cols], rows_o.at[r]
        else:
            src, dst = hid.at[0, r], hid.at[1, r]
        return remote(src, dst, core_s.at[kind, c], core_r.at[kind, c], other)

    def forward(c):
        arrived(NEEDS[c])
        if c == 0:
            load_w_in.wait()
        r = pl.ds(OFF[c], SIZE[c])
        go(core_copy(0, c))

        @pl.loop(0, HS // 256, unroll=True)
        def _(n):
            cols = pl.ds(al(n * 256, 256), 256)
            v = dot(rows[r, pl.ds(0, F)], w_in[:, cols])
            s = jax.nn.sigmoid(v)
            hid[0, r, cols] = (v * s).astype(BF16)
            slope[r, cols] = s * (1.0 + v * (1.0 - s))

        go(core_copy(1, c))

    def halves(c, way):
        h = SIZE[c] // 2
        return pl.ds(OFF[c] + way * h, h), pl.ds(OFF[c] // 2, h)

    def predict(c, rel):
        r = pl.ds(OFF[c], SIZE[c])
        part[rel, r] = dot(hid[0, r], w_out[:, quarter(t + rel)])

    def predict_first(c):
        if c == 0:
            load_w_out.wait()
        for way, rel in ((0, 3), (1, 1)):
            predict(c, rel)
            r, q = halves(c, way)
            sbuf[0, way, q] = part[rel, r].astype(BF16)
            go(rs(c, 0, way))

    def rs(c, s, way):
        _, q = halves(c, way)
        return remote(
            sbuf.at[s, way, q], rbuf.at[s, way, q], rs_s.at[c, s, way], rs_r.at[c, s, way],
            z_dev(1 + 2 * way),
        )

    def rs_step(c, s):
        for way in range(2):
            rs(c, s - 1, way).wait_recv()
            rel = (3 - s) if way == 0 else (1 + s)
            r, q = halves(c, way)
            sbuf[s, way, q] = (part[rel, r] + rbuf[s - 1, way, q].astype(F32)).astype(BF16)
            go(rs(c, s, way))

    def ag_copy(c, k, way, incoming):
        r, _ = halves(c, way if k != 1 else 1 - way)
        source = t if k < 2 else t + 3 - 2 * way
        if incoming:
            source = source + 3 - 2 * way
        ref = err.at[r, quarter(source)]
        return remote(ref, ref, ag_s.at[c, k, way], ag_r.at[c, k, way], z_dev(1 + 2 * way))

    def errors(c):
        for way in range(2):
            rs(c, 2, way).wait_recv()
            r, q = halves(c, way)
            pred = part[0, r] + rbuf[2, way, q].astype(F32)
            goal = rows[r, pl.ds(F, FQ)].astype(F32)
            err[r, quarter(t)] = ((pred - goal) * SCALE).astype(BF16)
            pred_b[r] = pred.astype(BF16)
            go(ag_copy(c, 0, way, False))
        for way in range(2):
            go(ag_copy(c, 1, way, False))

    def ag_forward(c):
        for way in range(2):
            ag_copy(c, 0, way, True).wait_recv()
            go(ag_copy(c, 2, way, False))

    def reward_send(c):
        for strip in CHUNKS[c]:
            half, dy, dx = int(strip[0] == "B"), int(strip[1]), int(strip[2])
            k = POS[strip] // ST
            src = pred_b.at[pl.ds(POS[strip], ST)]
            dst = gathered.at[m, pl.ds(ST * half, ST)]
            if (dy, dx) == (0, 0):
                pltpu.make_async_copy(src, dst, rwl_sem.at[half]).start()
            else:
                go(remote(src, dst, rw_s.at[k], rw_r.at[m, half], plane_dev(dy, dx)))

    def group_rows(g):
        c0, c1 = GROUPS[g][0], GROUPS[g][-1]
        return pl.ds(OFF[c0], OFF[c1] + SIZE[c1] - OFF[c0])

    def group_copy(kind, g):
        r = group_rows(g)
        if kind == 0:
            src, dst = err.at[r, other_cols], err_o.at[r]
        else:
            src, dst = pre.at[0, r], pre.at[1, r]
        return remote(src, dst, grp_s.at[kind, g], grp_r.at[kind, g], other)

    def back(g):
        for c in GROUPS[g]:
            for k in (1, 2):
                for way in range(2):
                    ag_copy(c, k, way, True).wait_recv()
        go(group_copy(0, g))
        r = group_rows(g)

        @pl.loop(0, HS // 256, unroll=True)
        def _(n):
            cols = pl.ds(al(n * 256, 256), 256)
            v = dot_nt(err[r], w_out[cols, :])
            pre[0, r, cols] = (v * slope[r, cols]).astype(BF16)

        go(group_copy(1, g))

    begun = set()

    def grad_out(g):
        for c in GROUPS[g]:
            core_copy(1, c).wait_recv()
        group_copy(0, g).wait_recv()
        r = group_rows(g)
        first = "out" not in begun
        begun.add("out")

        @pl.loop(0, HS // 256, unroll=True)
        def _(n):
            cols = pl.ds(al(n * 256, 256), 256)
            v = dot_tn(hid[0, r, cols], err[r, mine_cols]) + dot_tn(hid[1, r, cols], err_o[r])
            acc_out[0, cols, :] = v if first else acc_out[0, cols, :] + v

    def grad_in(g):
        for c in GROUPS[g]:
            core_copy(0, c).wait_recv()
        group_copy(1, g).wait_recv()
        r = group_rows(g)
        first = "in" not in begun
        begun.add("in")

        @pl.loop(0, FH // 256, unroll=True)
        def _(n):
            mine = pl.ds(al(b * FH + n * 256, 128), 256)
            cols = pl.ds(al(n * 256, 256), 256)
            v = dot_tn(rows[r, mine], pre[0, r]) + dot_tn(rows_o[r, cols], pre[1, r])
            acc_in[0, cols, :] = v if first else acc_in[0, cols, :] + v

    def spread_copy(d):
        return remote(
            spread.at[pl.ds(al(((t + d) % 4) * 16, 16), 16)],
            spread_r.at[d - 1],
            rz_s.at[d - 1],
            rz_r.at[d - 1],
            z_dev(d),
        )

    def reward_first():
        @pl.loop(1, MEMBERS)
        def _(d):
            s = (m + d) % MEMBERS
            for half in range(2):
                remote(
                    pred_b.at[pl.ds(0, ST)],
                    gathered.at[s, pl.ds(ST * half, ST)],
                    rw_s.at[2],
                    rw_r.at[s, half],
                    (b, s, t),
                ).wait_recv()

        for half in range(2):
            pltpu.make_async_copy(
                pred_b.at[pl.ds(ST * half, ST)],
                gathered.at[m, pl.ds(ST * half, ST)],
                rwl_sem.at[half],
            ).wait()

        total = jnp.zeros((64, 128), F32)
        for k in range(3):
            cols = pl.ds(128 * k, 128)
            mean = jnp.zeros((64, 128), F32)
            for s in range(MEMBERS):
                mean += gathered[s, :, cols].astype(F32)
            mean = mean * (1.0 / MEMBERS)
            for s in range(MEMBERS):
                dev = gathered[s, :, cols].astype(F32) - mean
                total += dev * dev
        spread[...] = total
        for d in range(1, 4):
            go(spread_copy(d))

    def reward_last():
        for d in range(1, 4):
            spread_copy(d).wait_recv()
        own = spread[pl.ds(al(t * 16, 16), 16)]
        for d in range(3):
            own += spread_r[d]
        reward_ref[...] = jnp.sum(own.T, axis=0, keepdims=True) * (1.0 / (MEMBERS * F))

    def sent(keep):
        while len(started) > keep:
            started.pop(0).wait_send()

    for step in ORDER:
        kind, k = step[0], int(step[1:])
        if kind == "P":
            send_hops(("p1", "p2"))
        elif kind == "X":
            arrived(RELAY[step][0])
            send_hops(RELAY[step][1])
        elif kind == "F":
            forward(k)
        elif kind == "G":
            predict_first(k)
        elif kind == "H":
            predict(k, 2)
            predict(k, 0)
        elif kind == "R":
            rs_step(k, 1)
        elif kind == "S":
            rs_step(k, 2)
        elif kind == "E":
            errors(k)
        elif kind == "A":
            ag_forward(k)
        elif kind == "W":
            reward_send(k)
        elif kind == "B":
            back(k)
        elif kind == "O":
            grad_out(k)
        elif kind == "I":
            grad_in(k)
        elif kind == "T":
            sent(16)
        elif step == "Y1":
            reward_first()
        else:
            reward_last()
    sent(0)


def per_device(rows_in, target, w_in, w_out):
    any_spec = pl.BlockSpec(memory_space=pl.ANY)
    vmem = pltpu.VMEM
    dma = pltpu.SemaphoreType.DMA
    reward, grad_in, grad_out = pl.pallas_call(
        kernel,
        out_shape=(
            vmem((1, 16), F32),
            vmem((1, FH, HS), F32),
            vmem((1, HS, FH), F32),
        ),
        in_specs=[any_spec] * 4,
        out_specs=(pl.BlockSpec(memory_space=pltpu.VMEM),) * 3,
        scratch_shapes=[
            vmem((F, HS), BF16),
            vmem((HS, F), BF16),
            vmem((R, W), BF16),
            vmem((R, FH), BF16),
            vmem((2, R, HS), BF16),
            vmem((R, HS), F32),
            vmem((4, R, FQ), F32),
            vmem((3, 2, R // 2, FQ), BF16),
            vmem((3, 2, R // 2, FQ), BF16),
            vmem((R, F), BF16),
            vmem((R, FH), BF16),
            vmem((2, R, HS), BF16),
            vmem((R, FQ), BF16),
            vmem((MEMBERS, 64, FQ), BF16),
            vmem((64, 128), F32),
            vmem((3, 16, 128), F32),
            dma((4,)),
            dma((3,)),
            dma((3,)),
            dma((len(HOPS),)),
            dma((len(HOPS),)),
            dma((NC, 3, 2)),
            dma((NC, 3, 2)),
            dma((NC, 3, 2)),
            dma((NC, 3, 2)),
            dma((2, NC)),
            dma((2, NC)),
            dma((2, NG)),
            dma((2, NG)),
            dma((len(STRIPS),)),
            dma((MEMBERS, 2)),
            dma((2,)),
            dma((3,)),
            dma((3,)),
        ],
        compiler_params=pltpu.CompilerParams(
            collective_id=0, has_side_effects=True, vmem_limit_bytes=54 * 1024 * 1024
        ),
        name="ensemble",
    )(rows_in, target, w_in, w_out)
    return reward.reshape(16), grad_in, grad_out


def solution(mesh):
    return jax.shard_map(
        per_device,
        mesh=mesh,
        in_specs=(
            P(("batch", "member", "tensor"), None),
            P(("batch", "member"), "tensor"),
            P("member", None, "tensor"),
            P("member", "tensor", None),
        ),
        out_specs=(
            P(("batch", "member", "tensor")),
            P("member", "batch", "tensor"),
            P("member", "tensor", "batch"),
        ),
        check_vma=False,
    )
```

time: 500 us -> 85.6 us (0.17)
  waiting for transfers between devices: 235 us -> 0 us
  blocking collectives: 203 us -> 0 us
  Pallas kernels: 0 us -> 80.7 us
  matrix products: 35.1 us -> 0 us
  between operations: 14.2 us -> 0.64 us
  other arithmetic: 5.53 us -> 0 us
    psum x1 -> x0, blocking collectives: 176 us -> none  [per_device(): spread = lax.psum(spread, ('member', 'tensor'))]
    all_gather x2 -> x0, waiting for transfers between devices: 112 us -> none  [the longest x1 72.5 us: per_device(): gathered = lax.all_gather(rows_in, ('member', 'tensor'), axis=0, tiled=True)]
    pallas_call x0 -> x1, Pallas kernels: none -> 80.7 us  [per_device(): pl.pallas_call(kernel, out_shape=(vmem((1, 16), F32), vmem((1, FH, HS), F...]
    reduce_scatter x3 -> x0, waiting for transfers between devices: 61.8 us -> none  [the longest x1 61.8 us: per_device(): lax.psum_scatter(partial_out, 'tensor', scatter_dimension=2, tiled=True)]
    psum x1 -> x0, waiting for transfers between devices: 60.7 us -> none  [per_device(): lax.psum(jnp.sum(predicted, 0).astype(jnp.bfloat16), 'member')]
    dot_general x4 -> x0, matrix products: 35.1 us -> none  [the longest x1 13.7 us: per_device(): jnp.einsum('gf,mgh->mfh', gathered, pre_grad, preferred_element_type=jnp....]
    all_gather x1 -> x0, blocking collectives: 27 us -> none  [per_device(): targets_here = lax.all_gather(target, 'member', axis=0, tiled=True)]
    convert_element_type x2 -> x0, other arithmetic: 5.53 us -> none  [the longest x1 3.16 us: per_device(): ((predicted - targets_here.astype(jnp.float32)[None]) * loss_scale).astyp...]
  transfers between devices with their start and end apart: 6 -> 0, of which waited for: 4 -> 0; matrix products, arithmetic and copies ran while one was open for 3% -> 0% of each run, Pallas kernels for 0% -> 0%
where the time goes in v3:
time: 85.6 us; the launch traced here: 85.2 us
  Pallas kernels  80.7 us (94%)
  local copies, waits for them, and re-layouts  3.84 us (4%)
    pallas_call x1, Pallas kernels, per_device(): pl.pallas_call(kernel, out_shape=(vmem((1, 16), F32), vmem((1, FH, HS), F...  80.7 us
    unnamed x3, local copies, waits for them, and re-layouts  3.84 us

profile of v3, /device:TPU:0, one launch (start us, length us, event | category | flops | bytes accessed | tf_op | source)
XLA Modules:
  0.0 85.2 jit_solution(9404633596610424853)
XLA Ops:
  0.6 80.7 %ensemble.1 = (f32[1,16]{1,0:T(1,128)S(1)}, f32[1,768,1024]{2,1,0:T(8,128)S(1)}, f32[1,1024,768]{2,1,0:T(8,128)S(1)}) custom-call(bf16[16,1536]{1,0:T(8,128)(2,1)} %rows_hbm.1, bf16[64,384]{1,0:T(8,128)(2,1)} %target_hbm.1, bf16[1,1536,1024]{2,1,0:T(8,128)(2,1)} %w_in_hbm.1, bf16[1,1024,1536]{2,1,0:T(8,128)(2,1)} %w_out_hbm.1), custom_call_target="tpu_custom_call" | custom-call | tf_op jit(solution)/shard_map/ensemble/pallas_call | solution.py:447
  81.4 0.5 copy.10
  81.9 1.7 %copy.11 = f32[1,768,1024]{2,1,0:T(8,128)} copy(f32[1,768,1024]{2,1,0:T(8,128)S(1)} %get-tuple-element.10) | data formatting | bytes 6291456
  83.5 1.7 %copy.12 = f32[1,1024,768]{2,1,0:T(8,128)} copy(f32[1,1024,768]{2,1,0:T(8,128)S(1)} %get-tuple-element.11) | data formatting | bytes 6291456

commit v4 on v3

--- a/solution.py
+++ b/solution.py
@@ -141,11 +141,8 @@
         pl.semaphore_signal(barrier, inc=1, device_id=z_dev(d), device_id_type=MESH)
     pl.semaphore_signal(barrier, inc=1, device_id=other, device_id_type=MESH)
 
-    @pl.loop(1, MEMBERS)
-    def _(d):
-        pl.semaphore_signal(
-            barrier, inc=1, device_id=(b, (m + d) % MEMBERS, t), device_id_type=MESH
-        )
+    for dy, dx in ((0, 1), (0, 3), (1, 0), (3, 0)):
+        pl.semaphore_signal(barrier, inc=1, device_id=plane_dev(dy, dx), device_id_type=MESH)
 
     own_rows = rows.at[pl.ds(al(t * 16, 16), 16), pl.ds(0, F)]
     load_rows = pltpu.make_async_copy(rows_hbm, own_rows, loc_sem.at[0])
@@ -158,15 +155,15 @@
     load_target.start()
     load_w_in.start()
     load_w_out.start()
-    pl.semaphore_wait(barrier, 3 + 1 + MEMBERS - 1)
-
+    pl.semaphore_wait(barrier, 3 + 1 + 4)
+
+    load_rows.wait()
     for d in (2, 1, 3):
-        go(remote(rows_hbm, own_rows, zg_s.at[d - 1], zg_r.at[d - 1], z_dev(d)))
-    load_rows.wait()
+        go(remote(own_rows, own_rows, zg_s.at[d - 1], zg_r.at[d - 1], z_dev(d)))
     load_target.wait()
     for d in (1, 3, 2):
         theirs = rows.at[pl.ds(al(((t + 4 - d) % 4) * 16, 16), 16), pl.ds(0, F)]
-        remote(rows_hbm, theirs, zg_s.at[d - 1], zg_r.at[d - 1], z_dev(d)).wait_recv()
+        remote(own_rows, theirs, zg_s.at[d - 1], zg_r.at[d - 1], z_dev(d)).wait_recv()
 
     def hop(k):
         _, first, skip, n, land, (dy, dx) = HOPS[k]

time: 85.6 us -> 84.6 us (0.988)
  no operation moved by 1% of the time
where the time goes in v4:
time: 84.6 us; the launch traced here: 84.4 us
  Pallas kernels  80 us (95%)
  local copies, waits for them, and re-layouts  3.84 us (5%)
    pallas_call x1, Pallas kernels, per_device(): pl.pallas_call(kernel, out_shape=(vmem((1, 16), F32), vmem((1, FH, HS), F...  80 us
    unnamed x3, local copies, waits for them, and re-layouts  3.84 us

profile of v4, /device:TPU:0, one launch (start us, length us, event | category | flops | bytes accessed | tf_op | source)
XLA Modules:
  0.0 84.4 jit_solution(2185155699860189903)
XLA Ops:
  0.6 80.0 %ensemble.1 = (f32[1,16]{1,0:T(1,128)S(1)}, f32[1,768,1024]{2,1,0:T(8,128)S(1)}, f32[1,1024,768]{2,1,0:T(8,128)S(1)}) custom-call(bf16[16,1536]{1,0:T(8,128)(2,1)} %rows_hbm.1, bf16[64,384]{1,0:T(8,128)(2,1)} %target_hbm.1, bf16[1,1536,1024]{2,1,0:T(8,128)(2,1)} %w_in_hbm.1, bf16[1,1024,1536]{2,1,0:T(8,128)(2,1)} %w_out_hbm.1), custom_call_target="tpu_custom_call" | custom-call | tf_op jit(solution)/shard_map/ensemble/pallas_call | solution.py:444
  80.6 0.5 copy.10
  81.1 1.7 %copy.11 = f32[1,768,1024]{2,1,0:T(8,128)} copy(f32[1,768,1024]{2,1,0:T(8,128)S(1)} %get-tuple-element.10) | data formatting | bytes 6291456
  82.8 1.7 %copy.12 = f32[1,1024,768]{2,1,0:T(8,128)} copy(f32[1,1024,768]{2,1,0:T(8,128)S(1)} %get-tuple-element.11) | data formatting | bytes 6291456

commit v5 on v4

--- a/solution.py
+++ b/solution.py
@@ -35,6 +35,9 @@
 NC = len(CHUNKS)
 GROUPS = ((0, 1, 2), (3,), (4,), (5, 6))
 NG = len(GROUPS)
+LAST = GROUPS[-1]
+LB = OFF[LAST[0]]
+LN = R - LB
 
 HOPS = (
     ("p1", "A00", 0, 32, "A03", (0, 1)),
@@ -76,10 +79,10 @@
 ORDER = (
     "P1", "F0", "G0", "H0", "R0", "X1", "F1", "G1", "S0", "F2", "G2", "H2", "H1", "R1", "X2",
     "E0", "R2", "S1", "A0", "F3", "S2", "X3", "G3", "E1", "F4", "E2", "G4", "H3", "F5", "X4",
-    "H5", "H4", "G5", "W1", "R3", "A2", "R4", "F6", "A1", "H6", "S3", "G6", "W2", "S4", "R5",
-    "B0", "E3", "W0", "R6", "A3", "S5", "I0", "S6", "E4", "O0", "E5", "W5", "E6", "B1", "A4",
-    "W4", "W3", "A5", "O1", "A6", "W6", "I1", "B2", "T1", "B3", "Y1", "O2", "I2", "I3", "O3",
-    "Y2",
+    "H5", "H4", "G5", "W0", "W1", "R3", "A2", "R4", "F6", "A1", "H6", "S3", "G6", "W2", "S4",
+    "R5", "T3", "B0", "E3", "R6", "A3", "W3", "S5", "T3", "I0", "S6", "E4", "W4", "O0", "E5",
+    "W5", "E6", "W6", "T3", "B1", "A4", "A5", "O1", "A6", "I1", "T2", "B2", "Y1", "B3", "O2",
+    "I2", "Y2", "Z1",
 )
 
 
@@ -97,7 +100,7 @@
 
 def kernel(
     rows_hbm, target_hbm, w_in_hbm, w_out_hbm,
-    reward_ref, acc_in, acc_out,
+    reward_ref, acc_in, acc_out, hid_l, pre_l, err_l, rows_l,
     w_in, w_out, rows, rows_o, hid, slope, part, sbuf, rbuf, err, err_o, pre,
     pred_b, gathered, spread, spread_r,
     loc_sem, zg_s, zg_r, xy_s, xy_r, rs_s, rs_r, ag_s, ag_r, core_s, core_r, grp_s, grp_r,
@@ -191,12 +194,19 @@
                 if HOPS[k][0] == name:
                     go(hop(k))
 
+    def hid_of(whose, c):
+        if c in LAST:
+            return hid_l.at[whose, pl.ds(OFF[c] - LB, SIZE[c])]
+        return hid.at[whose, pl.ds(OFF[c], SIZE[c])]
+
     def core_copy(kind, c):
         r = pl.ds(OFF[c], SIZE[c])
-        if kind == 0:
+        if kind == 1:
+            src, dst = hid_of(0, c), hid_of(1, c)
+        elif c in LAST:
+            src, dst = rows.at[r, other_cols], rows_l.at[1, pl.ds(OFF[c] - LB, SIZE[c])]
+        else:
             src, dst = rows.at[r, other_cols], rows_o.at[r]
-        else:
-            src, dst = hid.at[0, r], hid.at[1, r]
         return remote(src, dst, core_s.at[kind, c], core_r.at[kind, c], other)
 
     def forward(c):
@@ -205,13 +215,14 @@
             load_w_in.wait()
         r = pl.ds(OFF[c], SIZE[c])
         go(core_copy(0, c))
+        out = hid_of(0, c)
 
         @pl.loop(0, HS // 256, unroll=True)
         def _(n):
             cols = pl.ds(al(n * 256, 256), 256)
             v = dot(rows[r, pl.ds(0, F)], w_in[:, cols])
             s = jax.nn.sigmoid(v)
-            hid[0, r, cols] = (v * s).astype(BF16)
+            out[:, cols] = (v * s).astype(BF16)
             slope[r, cols] = s * (1.0 + v * (1.0 - s))
 
         go(core_copy(1, c))
@@ -222,7 +233,7 @@
 
     def predict(c, rel):
         r = pl.ds(OFF[c], SIZE[c])
-        part[rel, r] = dot(hid[0, r], w_out[:, quarter(t + rel)])
+        part[rel, r] = dot(hid_of(0, c)[...], w_out[:, quarter(t + rel)])
 
     def predict_first(c):
         if c == 0:
@@ -290,8 +301,11 @@
 
     def group_copy(kind, g):
         r = group_rows(g)
+        last = g == NG - 1
         if kind == 0:
-            src, dst = err.at[r, other_cols], err_o.at[r]
+            src, dst = err.at[r, other_cols], err_l.at[1] if last else err_o.at[r]
+        elif last:
+            src, dst = pre_l.at[0], pre_l.at[1]
         else:
             src, dst = pre.at[0, r], pre.at[1, r]
         return remote(src, dst, grp_s.at[kind, g], grp_r.at[kind, g], other)
@@ -303,14 +317,25 @@
                     ag_copy(c, k, way, True).wait_recv()
         go(group_copy(0, g))
         r = group_rows(g)
+        out = pre_l.at[0] if g == NG - 1 else pre.at[0, r]
 
         @pl.loop(0, HS // 256, unroll=True)
         def _(n):
             cols = pl.ds(al(n * 256, 256), 256)
             v = dot_nt(err[r], w_out[cols, :])
-            pre[0, r, cols] = (v * slope[r, cols]).astype(BF16)
+            out[:, cols] = (v * slope[r, cols]).astype(BF16)
 
         go(group_copy(1, g))
+        if g == NG - 1:
+            err_l[0] = err[r, mine_cols]
+            rows_l[0] = rows[r, mine_cols]
+
+    def last_arrived():
+        for c in LAST:
+            core_copy(0, c).wait_recv()
+            core_copy(1, c).wait_recv()
+        group_copy(0, NG - 1).wait_recv()
+        group_copy(1, NG - 1).wait_recv()
 
     begun = set()
 
@@ -326,7 +351,7 @@
         def _(n):
             cols = pl.ds(al(n * 256, 256), 256)
             v = dot_tn(hid[0, r, cols], err[r, mine_cols]) + dot_tn(hid[1, r, cols], err_o[r])
-            acc_out[0, cols, :] = v if first else acc_out[0, cols, :] + v
+            acc_out[cols, :] = v if first else acc_out[cols, :] + v
 
     def grad_in(g):
         for c in GROUPS[g]:
@@ -341,7 +366,7 @@
             mine = pl.ds(al(b * FH + n * 256, 128), 256)
             cols = pl.ds(al(n * 256, 256), 256)
             v = dot_tn(rows[r, mine], pre[0, r]) + dot_tn(rows_o[r, cols], pre[1, r])
-            acc_in[0, cols, :] = v if first else acc_in[0, cols, :] + v
+            acc_in[cols, :] = v if first else acc_in[cols, :] + v
 
     def spread_copy(d):
         return remote(
@@ -429,7 +454,9 @@
         elif kind == "I":
             grad_in(k)
         elif kind == "T":
-            sent(16)
+            sent(10 * k)
+        elif kind == "Z":
+            last_arrived()
         elif step == "Y1":
             reward_first()
         else:
@@ -437,32 +464,63 @@
     sent(0)
 
 
+def finish(
+    reward, acc_in, acc_out, hid_l, pre_l, err_l, rows_l,
+    reward_ref, grad_in_hbm, grad_out_hbm, tile_in, tile_out, sem,
+):
+    reward_ref[...] = reward[...]
+    copies = []
+    for n in range(HS // 256):
+        cols = pl.ds(n * 256, 256)
+        v = dot_tn(hid_l[0, :, cols], err_l[0]) + dot_tn(hid_l[1, :, cols], err_l[1])
+        tile_out[cols, :] = acc_out[cols, :] + v
+        copies.append(
+            pltpu.make_async_copy(tile_out.at[cols], grad_out_hbm.at[0, cols], sem.at[n])
+        )
+        copies[-1].start()
+    for n in range(FH // 256):
+        cols = pl.ds(n * 256, 256)
+        v = dot_tn(rows_l[0, :, cols], pre_l[0]) + dot_tn(rows_l[1, :, cols], pre_l[1])
+        tile_in[cols, :] = acc_in[cols, :] + v
+        copies.append(
+            pltpu.make_async_copy(tile_in.at[cols], grad_in_hbm.at[0, cols], sem.at[4 + n])
+        )
+        copies[-1].start()
+    for copy in copies:
+        copy.wait()
+
+
 def per_device(rows_in, target, w_in, w_out):
     any_spec = pl.BlockSpec(memory_space=pl.ANY)
+    vmem_spec = pl.BlockSpec(memory_space=pltpu.VMEM)
     vmem = pltpu.VMEM
     dma = pltpu.SemaphoreType.DMA
-    reward, grad_in, grad_out = pl.pallas_call(
+    parts = pl.pallas_call(
         kernel,
         out_shape=(
             vmem((1, 16), F32),
-            vmem((1, FH, HS), F32),
-            vmem((1, HS, FH), F32),
+            vmem((FH, HS), F32),
+            vmem((HS, FH), F32),
+            vmem((2, LN, HS), BF16),
+            vmem((2, LN, HS), BF16),
+            vmem((2, LN, FH), BF16),
+            vmem((2, LN, FH), BF16),
         ),
         in_specs=[any_spec] * 4,
-        out_specs=(pl.BlockSpec(memory_space=pltpu.VMEM),) * 3,
+        out_specs=(vmem_spec,) * 7,
         scratch_shapes=[
             vmem((F, HS), BF16),
             vmem((HS, F), BF16),
             vmem((R, W), BF16),
-            vmem((R, FH), BF16),
-            vmem((2, R, HS), BF16),
+            vmem((LB, FH), BF16),
+            vmem((2, LB, HS), BF16),
             vmem((R, HS), F32),
             vmem((4, R, FQ), F32),
             vmem((3, 2, R // 2, FQ), BF16),
             vmem((3, 2, R // 2, FQ), BF16),
             vmem((R, F), BF16),
-            vmem((R, FH), BF16),
-            vmem((2, R, HS), BF16),
+            vmem((LB, FH), BF16),
+            vmem((2, LB, HS), BF16),
             vmem((R, FQ), BF16),
             vmem((MEMBERS, 64, FQ), BF16),
             vmem((64, 128), F32),
@@ -487,10 +545,23 @@
             dma((3,)),
         ],
         compiler_params=pltpu.CompilerParams(
-            collective_id=0, has_side_effects=True, vmem_limit_bytes=54 * 1024 * 1024
+            collective_id=0, has_side_effects=True, vmem_limit_bytes=46 * 1024 * 1024
         ),
         name="ensemble",
     )(rows_in, target, w_in, w_out)
+    reward, grad_in, grad_out = pl.pallas_call(
+        finish,
+        out_shape=(
+            jax.ShapeDtypeStruct((1, 16), F32),
+            jax.ShapeDtypeStruct((1, FH, HS), F32),
+            jax.ShapeDtypeStruct((1, HS, FH), F32),
+        ),
+        in_specs=[vmem_spec] * 7,
+        out_specs=(vmem_spec, any_spec, any_spec),
+        scratch_shapes=[vmem((FH, HS), F32), vmem((HS, FH), F32), dma((7,))],
+        compiler_params=pltpu.CompilerParams(vmem_limit_bytes=24 * 1024 * 1024),
+        name="finish",
+    )(*parts)
     return reward.reshape(16), grad_in, grad_out
 
 

time: 84.6 us -> 81.4 us (0.962)
  local copies, waits for them, and re-layouts: 3.84 us -> 0 us
    unnamed x3 -> x0, local copies, waits for them, and re-layouts: 3.84 us -> none
    pallas_call x1 -> x2, Pallas kernels: 80 us -> 80.1 us  [the longest x1 76.4 us: per_device(): pl.pallas_call(kernel, out_shape=(vmem((1, 16), F32), vmem((FH, HS), F32)...]
where the time goes in v5:
time: 81.4 us; the launch traced here: 80.9 us
  Pallas kernels  80.1 us (98%)
  between operations  0.82 us (1%)
    pallas_call x1, Pallas kernels, per_device(): pl.pallas_call(kernel, out_shape=(vmem((1, 16), F32), vmem((FH, HS), F32)...  76.4 us
    pallas_call x1, Pallas kernels, per_device(): pl.pallas_call(finish, out_shape=(jax.ShapeDtypeStruct((1, 16), F32), jax...  3.72 us

profile of v5, /device:TPU:0, one launch (start us, length us, event | category | flops | bytes accessed | tf_op | source)
XLA Modules:
  0.0 80.9 jit_solution(5913249768314923348)
XLA Ops:
  0.6 76.4 %ensemble.1 = (f32[1,16]{1,0:T(1,128)S(1)}, f32[768,1024]{1,0:T(8,128)S(1)}, f32[1024,768]{1,0:T(8,128)S(1)}, bf16[2,256,1024]{2,1,0:T(8,128)(2,1)S(1)}, bf16[2,...) custom-call(bf16[16,1536]{1,0:T(8,128)(2,1)} %rows_hbm.1, ...), custom_call_target="tpu_custom_call" | custom-call | tf_op jit(solution)/shard_map/ensemble/pallas_call | solution.py:498
  77.0 3.7 %finish.1 = (f32[1,16]{1,0:T(1,128)}, f32[1,768,1024]{2,1,0:T(8,128)}, f32[1,1024,768]{2,1,0:T(8,128)}) custom-call(f32[1,16]{1,0:T(1,128)S(1)} %get-tuple-element.13.reward, f32[768,1024]{1,0:T(8,128)S(1)} %get-tuple-element.14.acc_in, f32[1024,768]{1,0:T(8,128)S(1)} %get-tuple-element.15.acc_out, bf16[2,256,1024]{2,1,0:T(8,128)(2,1)S(1)} %get-tuple-element.16.hid_l, ...), custom_call_target="tpu_custom_call" | custom-call | tf_op jit(solution)/shard_map/finish/pallas_call | solution.py:552

commit v6 on v5

--- a/solution.py
+++ b/solution.py
@@ -14,7 +14,6 @@
 FQ = F // 4
 HS = 1024
 R = 1024
-W = F + FQ
 ST = 32
 MEMBERS = 16
 SCALE = 2048.0**-0.5
@@ -69,20 +68,26 @@
     ("q6", "B23", 0, 32, "B22", (0, 1)),
     ("q6", "B11", 0, 32, "B12", (0, 3)),
 )
+HOPS += tuple((h[0].upper(),) + h[1:] for h in HOPS)
+GOALS = ((), ("P1",), ("P2",), ("Q3",), ("D", "Q4"), ("Q5",), ("Q6",))
 NEEDS = ((), ("p1",), ("p2",), ("q3",), ("d", "q4"), ("q5",), ("q6",))
 RELAY = {
     "X1": (("p1",), ("d", "q3")),
     "X2": (("d",), ("q4",)),
     "X3": (("p2", "q3"), ("q5",)),
     "X4": (("q3", "q4"), ("q6",)),
+    "X5": ((), ("P1", "P2")),
+    "X6": (("P1",), ("D", "Q3")),
+    "X7": (("D", "P2", "Q3"), ("Q4", "Q5")),
+    "X8": (("Q4",), ("Q6",)),
 }
 ORDER = (
-    "P1", "F0", "G0", "H0", "R0", "X1", "F1", "G1", "S0", "F2", "G2", "H2", "H1", "R1", "X2",
-    "E0", "R2", "S1", "A0", "F3", "S2", "X3", "G3", "E1", "F4", "E2", "G4", "H3", "F5", "X4",
-    "H5", "H4", "G5", "W0", "W1", "R3", "A2", "R4", "F6", "A1", "H6", "S3", "G6", "W2", "S4",
-    "R5", "T3", "B0", "E3", "R6", "A3", "W3", "S5", "T3", "I0", "S6", "E4", "W4", "O0", "E5",
-    "W5", "E6", "W6", "T3", "B1", "A4", "A5", "O1", "A6", "I1", "T2", "B2", "Y1", "B3", "O2",
-    "I2", "Y2", "Z1",
+    "P1", "F0", "G0", "H0", "R0", "X1", "X5", "F1", "G1", "S0", "F2", "G2", "H2", "H1", "R1",
+    "X2", "E0", "R2", "S1", "A0", "F3", "S2", "X3", "G3", "E1", "X6", "F4", "E2", "G4", "H3",
+    "F5", "X4", "H5", "H4", "G5", "W0", "W1", "R3", "A2", "X7", "R4", "F6", "A1", "H6", "S3",
+    "X8", "G6", "W2", "S4", "R5", "T3", "B0", "E3", "R6", "A3", "W3", "S5", "T3", "I0", "S6",
+    "E4", "W4", "O0", "E5", "W5", "E6", "W6", "T3", "B1", "A4", "A5", "O1", "A6", "I1", "T2",
+    "B2", "Y1", "B3", "O2", "I2", "Y2", "Z1",
 )
 
 
@@ -101,7 +106,7 @@
 def kernel(
     rows_hbm, target_hbm, w_in_hbm, w_out_hbm,
     reward_ref, acc_in, acc_out, hid_l, pre_l, err_l, rows_l,
-    w_in, w_out, rows, rows_o, hid, slope, part, sbuf, rbuf, err, err_o, pre,
+    w_in, w_out, rows, goal, rows_o, hid, slope, part, sbuf, rbuf, err, err_o, pre,
     pred_b, gathered, spread, spread_r,
     loc_sem, zg_s, zg_r, xy_s, xy_r, rs_s, rs_r, ag_s, ag_r, core_s, core_r, grp_s, grp_r,
     rw_s, rw_r, rwl_sem, rz_s, rz_r,
@@ -147,10 +152,10 @@
     for dy, dx in ((0, 1), (0, 3), (1, 0), (3, 0)):
         pl.semaphore_signal(barrier, inc=1, device_id=plane_dev(dy, dx), device_id_type=MESH)
 
-    own_rows = rows.at[pl.ds(al(t * 16, 16), 16), pl.ds(0, F)]
+    own_rows = rows.at[pl.ds(al(t * 16, 16), 16)]
     load_rows = pltpu.make_async_copy(rows_hbm, own_rows, loc_sem.at[0])
     load_target = pltpu.make_async_copy(
-        target_hbm, rows.at[pl.ds(0, 64), pl.ds(F, FQ)], loc_sem.at[1]
+        target_hbm, goal.at[pl.ds(0, 64)], loc_sem.at[1]
     )
     load_w_in = pltpu.make_async_copy(w_in_hbm.at[0], w_in, loc_sem.at[2])
     load_w_out = pltpu.make_async_copy(w_out_hbm.at[0], w_out, loc_sem.at[3])
@@ -163,16 +168,16 @@
     load_rows.wait()
     for d in (2, 1, 3):
         go(remote(own_rows, own_rows, zg_s.at[d - 1], zg_r.at[d - 1], z_dev(d)))
-    load_target.wait()
     for d in (1, 3, 2):
-        theirs = rows.at[pl.ds(al(((t + 4 - d) % 4) * 16, 16), 16), pl.ds(0, F)]
+        theirs = rows.at[pl.ds(al(((t + 4 - d) % 4) * 16, 16), 16)]
         remote(own_rows, theirs, zg_s.at[d - 1], zg_r.at[d - 1], z_dev(d)).wait_recv()
 
     def hop(k):
-        _, first, skip, n, land, (dy, dx) = HOPS[k]
+        name, first, skip, n, land, (dy, dx) = HOPS[k]
+        of = goal if name.isupper() else rows
         return remote(
-            rows.at[pl.ds(POS[first] + skip, n)],
-            rows.at[pl.ds(POS[land] + skip, n)],
+            of.at[pl.ds(POS[first] + skip, n)],
+            of.at[pl.ds(POS[land] + skip, n)],
             xy_s.at[k],
             xy_r.at[k],
             plane_dev(dy, dx),
@@ -220,7 +225,7 @@
         @pl.loop(0, HS // 256, unroll=True)
         def _(n):
             cols = pl.ds(al(n * 256, 256), 256)
-            v = dot(rows[r, pl.ds(0, F)], w_in[:, cols])
+            v = dot(rows[r], w_in[:, cols])
             s = jax.nn.sigmoid(v)
             out[:, cols] = (v * s).astype(BF16)
             slope[r, cols] = s * (1.0 + v * (1.0 - s))
@@ -268,12 +273,12 @@
         return remote(ref, ref, ag_s.at[c, k, way], ag_r.at[c, k, way], z_dev(1 + 2 * way))
 
     def errors(c):
+        arrived(GOALS[c])
         for way in range(2):
             rs(c, 2, way).wait_recv()
             r, q = halves(c, way)
             pred = part[0, r] + rbuf[2, way, q].astype(F32)
-            goal = rows[r, pl.ds(F, FQ)].astype(F32)
-            err[r, quarter(t)] = ((pred - goal) * SCALE).astype(BF16)
+            err[r, quarter(t)] = ((pred - goal[r].astype(F32)) * SCALE).astype(BF16)
             pred_b[r] = pred.astype(BF16)
             go(ag_copy(c, 0, way, False))
         for way in range(2):
@@ -428,6 +433,8 @@
         if kind == "P":
             send_hops(("p1", "p2"))
         elif kind == "X":
+            if step == "X5":
+                load_target.wait()
             arrived(RELAY[step][0])
             send_hops(RELAY[step][1])
         elif kind == "F":
@@ -511,7 +518,8 @@
         scratch_shapes=[
             vmem((F, HS), BF16),
             vmem((HS, F), BF16),
-            vmem((R, W), BF16),
+            vmem((R, F), BF16),
+            vmem((R, FQ), BF16),
             vmem((LB, FH), BF16),
             vmem((2, LB, HS), BF16),
             vmem((R, HS), F32),

time: 81.4 us -> 80.8 us (level)
  no operation moved by 1% of the time
where the time goes in v6:
time: 80.8 us; the launch traced here: 80.7 us
  Pallas kernels  79.9 us (99%)
  between operations  0.82 us (1%)
    pallas_call x1, Pallas kernels, per_device(): pl.pallas_call(kernel, out_shape=(vmem((1, 16), F32), vmem((FH, HS), F32)...  76.2 us
    pallas_call x1, Pallas kernels, per_device(): pl.pallas_call(finish, out_shape=(jax.ShapeDtypeStruct((1, 16), F32), jax...  3.72 us

profile of v6, /device:TPU:0, one launch (start us, length us, event | category | flops | bytes accessed | tf_op | source)
XLA Modules:
  0.0 80.7 jit_solution(11590350708840831664)
XLA Ops:
  0.6 76.2 %ensemble.1 = (f32[1,16]{1,0:T(1,128)S(1)}, f32[768,1024]{1,0:T(8,128)S(1)}, f32[1024,768]{1,0:T(8,128)S(1)}, bf16[2,256,1024]{2,1,0:T(8,128)(2,1)S(1)}, bf16[2,...) custom-call(bf16[16,1536]{1,0:T(8,128)(2,1)} %rows_hbm.1, ...), custom_call_target="tpu_custom_call" | custom-call | tf_op jit(solution)/shard_map/ensemble/pallas_call | solution.py:505
  76.8 3.7 %finish.1 = (f32[1,16]{1,0:T(1,128)}, f32[1,768,1024]{2,1,0:T(8,128)}, f32[1,1024,768]{2,1,0:T(8,128)}) custom-call(f32[1,16]{1,0:T(1,128)S(1)} %get-tuple-element.13.reward, f32[768,1024]{1,0:T(8,128)S(1)} %get-tuple-element.14.acc_in, f32[1024,768]{1,0:T(8,128)S(1)} %get-tuple-element.15.acc_out, bf16[2,256,1024]{2,1,0:T(8,128)(2,1)S(1)} %get-tuple-element.16.hid_l, ...), custom_call_target="tpu_custom_call" | custom-call | tf_op jit(solution)/shard_map/finish/pallas_call | solution.py:560

commit v7 on v6

--- a/solution.py
+++ b/solution.py
@@ -473,10 +473,10 @@
 
 def finish(
     reward, acc_in, acc_out, hid_l, pre_l, err_l, rows_l,
-    reward_ref, grad_in_hbm, grad_out_hbm, tile_in, tile_out, sem,
+    reward_hbm, grad_in_hbm, grad_out_hbm, tile_in, tile_out, sem,
 ):
-    reward_ref[...] = reward[...]
-    copies = []
+    copies = [pltpu.make_async_copy(reward, reward_hbm, sem.at[7])]
+    copies[0].start()
     for n in range(HS // 256):
         cols = pl.ds(n * 256, 256)
         v = dot_tn(hid_l[0, :, cols], err_l[0]) + dot_tn(hid_l[1, :, cols], err_l[1])
@@ -565,8 +565,8 @@
             jax.ShapeDtypeStruct((1, HS, FH), F32),
         ),
         in_specs=[vmem_spec] * 7,
-        out_specs=(vmem_spec, any_spec, any_spec),
-        scratch_shapes=[vmem((FH, HS), F32), vmem((HS, FH), F32), dma((7,))],
+        out_specs=(any_spec,) * 3,
+        scratch_shapes=[vmem((FH, HS), F32), vmem((HS, FH), F32), dma((8,))],
         compiler_params=pltpu.CompilerParams(vmem_limit_bytes=24 * 1024 * 1024),
         name="finish",
     )(*parts)

time: 80.8 us -> 80.3 us (level)
  no operation moved by 1% of the time
where the time goes in v7:
time: 80.3 us; the launch traced here: 80.2 us
  Pallas kernels  79.4 us (99%)
  between operations  0.82 us (1%)
    pallas_call x1, Pallas kernels, per_device(): pl.pallas_call(kernel, out_shape=(vmem((1, 16), F32), vmem((FH, HS), F32)...  76.2 us
    pallas_call x1, Pallas kernels, per_device(): pl.pallas_call(finish, out_shape=(jax.ShapeDtypeStruct((1, 16), F32), jax...  3.22 us

profile of v7, /device:TPU:0, one launch (start us, length us, event | category | flops | bytes accessed | tf_op | source)
XLA Modules:
  0.0 80.2 jit_solution(12308747903096623888)
XLA Ops:
  0.6 76.2 %ensemble.1 = (f32[1,16]{1,0:T(1,128)S(1)}, f32[768,1024]{1,0:T(8,128)S(1)}, f32[1024,768]{1,0:T(8,128)S(1)}, bf16[2,256,1024]{2,1,0:T(8,128)(2,1)S(1)}, bf16[2,...) custom-call(bf16[16,1536]{1,0:T(8,128)(2,1)} %rows_hbm.1, ...), custom_call_target="tpu_custom_call" | custom-call | tf_op jit(solution)/shard_map/ensemble/pallas_call | solution.py:505
  76.8 3.2 %finish.1 = (f32[1,16]{1,0:T(1,128)}, f32[1,768,1024]{2,1,0:T(8,128)}, f32[1,1024,768]{2,1,0:T(8,128)}) custom-call(f32[1,16]{1,0:T(1,128)S(1)} %get-tuple-element.13.reward, f32[768,1024]{1,0:T(8,128)S(1)} %get-tuple-element.14.acc_in, f32[1024,768]{1,0:T(8,128)S(1)} %get-tuple-element.15.acc_out, bf16[2,256,1024]{2,1,0:T(8,128)(2,1)S(1)} %get-tuple-element.16.hid_l, ...), custom_call_target="tpu_custom_call" | custom-call | tf_op jit(solution)/shard_map/finish/pallas_call | solution.py:560

commit v8 on v7

--- a/solution.py
+++ b/solution.py
@@ -82,7 +82,7 @@
     "X8": (("Q4",), ("Q6",)),
 }
 ORDER = (
-    "P1", "F0", "G0", "H0", "R0", "X1", "X5", "F1", "G1", "S0", "F2", "G2", "H2", "H1", "R1",
+    "P1", "F0", "G0", "H0", "R0", "X1", "F1", "G1", "X5", "S0", "F2", "G2", "H2", "H1", "R1",
     "X2", "E0", "R2", "S1", "A0", "F3", "S2", "X3", "G3", "E1", "X6", "F4", "E2", "G4", "H3",
     "F5", "X4", "H5", "H4", "G5", "W0", "W1", "R3", "A2", "X7", "R4", "F6", "A1", "H6", "S3",
     "X8", "G6", "W2", "S4", "R5", "T3", "B0", "E3", "R6", "A3", "W3", "S5", "T3", "I0", "S6",

time: 80.3 us -> 80.3 us (level)
  no operation moved by 1% of the time
where the time goes in v8:
time: 80.3 us; the launch traced here: 80.1 us
  Pallas kernels  79.3 us (99%)
  between operations  0.82 us (1%)
    pallas_call x1, Pallas kernels, per_device(): pl.pallas_call(kernel, out_shape=(vmem((1, 16), F32), vmem((FH, HS), F32)...  76.1 us
    pallas_call x1, Pallas kernels, per_device(): pl.pallas_call(finish, out_shape=(jax.ShapeDtypeStruct((1, 16), F32), jax...  3.22 us

profile of v8, /device:TPU:0, one launch (start us, length us, event | category | flops | bytes accessed | tf_op | source)
XLA Modules:
  0.0 80.1 jit_solution(800242525829040352)
XLA Ops:
  0.6 76.1 %ensemble.1 = (f32[1,16]{1,0:T(1,128)S(1)}, f32[768,1024]{1,0:T(8,128)S(1)}, f32[1024,768]{1,0:T(8,128)S(1)}, bf16[2,256,1024]{2,1,0:T(8,128)(2,1)S(1)}, bf16[2,...) custom-call(bf16[16,1536]{1,0:T(8,128)(2,1)} %rows_hbm.1, ...), custom_call_target="tpu_custom_call" | custom-call | tf_op jit(solution)/shard_map/ensemble/pallas_call | solution.py:505
  76.7 3.2 %finish.1 = (f32[1,16]{1,0:T(1,128)}, f32[1,768,1024]{2,1,0:T(8,128)}, f32[1,1024,768]{2,1,0:T(8,128)}) custom-call(f32[1,16]{1,0:T(1,128)S(1)} %get-tuple-element.13.reward, f32[768,1024]{1,0:T(8,128)S(1)} %get-tuple-element.14.acc_in, f32[1024,768]{1,0:T(8,128)S(1)} %get-tuple-element.15.acc_out, bf16[2,256,1024]{2,1,0:T(8,128)(2,1)S(1)} %get-tuple-element.16.hid_l, ...), custom_call_target="tpu_custom_call" | custom-call | tf_op jit(solution)/shard_map/finish/pallas_call | solution.py:560
